TPU v7x, 32 devices: a whole 2x2x4 slice. The times are simulated.
32 devices in a mesh: blk: 4 (over y, x), batch: 8 (over z, core).
Axes of the slice: x: 2, y: 2, z: 4, core: 2. Of those that a mesh axis runs over, the one named last changes fastest.
Arguments:
- inputs: bfloat16 [32, 512, 768], P('batch', 'blk'), may hold values from -6 to 6
- lengths: int32 [32], P('batch'), may hold values from 64 to 512, as said below
- positions: int32 [32, 80], P('batch'), may hold values from 0 to 511, as said below
- counts: int32 [32], P('batch'), may hold values from 40 to 80, as said below
- token_ids: int32 [32, 80], P('batch'), may hold values from 0 to 15359
- table: bfloat16 [15360, 768], replicated, may hold values from -6 to 6
- w_query: bfloat16 [768, 768], replicated, may hold values from -0.3125 to 0.3125
- b_query: bfloat16 [768], replicated, may hold values from -1.75 to 1.75
- w_key: bfloat16 [768, 768], replicated, may hold values from -0.21875 to 0.21875
- w_value: bfloat16 [768, 768], replicated, may hold values from -0.21875 to 0.21875
- b_value: bfloat16 [768], replicated, may hold values from -0.625 to 0.625
- w_out: bfloat16 [768, 768], replicated, may hold values from -1.75 to 1.75
- b_out: bfloat16 [768], replicated, may hold values from -3 to 3
- gain_one: bfloat16 [768], replicated, may hold values from 0.5 to 1.5
- shift_one: bfloat16 [768], replicated, may hold values from -1.75 to 1.75
- w_up: bfloat16 [768, 3072], replicated, may hold values from -0.21875 to 0.21875
- b_up: bfloat16 [3072], replicated, may hold values from -3 to 3
- w_down: bfloat16 [3072, 768], replicated, may hold values from -0.109375 to 0.109375
- b_down: bfloat16 [768], replicated, may hold values from -3 to 3
- gain_two: bfloat16 [768], replicated, may hold values from 0.5 to 1.5
- shift_two: bfloat16 [768], replicated, may hold values from -1.75 to 1.75
- cotangent: bfloat16 [32, 512, 768], P('batch', 'blk'), may hold values from -8 to 8
Outputs:
- outputs: bfloat16 [32, 512, 768], P('batch', 'blk')
- d_inputs: bfloat16 [32, 512, 768], P('batch', 'blk')
- grad_query: float32 [768, 768], P('batch')
- grad_query_bias: float32 [768], P('batch')
- grad_key: float32 [768, 768], P('batch')
- grad_value: float32 [768, 768], P('batch')
- grad_value_bias: float32 [768], P('batch')
- grad_out: float32 [768, 768], P('batch')
- grad_out_bias: float32 [768], P('batch')
- grad_gain_one: float32 [768], P('batch')
- grad_shift_one: float32 [768], P('batch')
- grad_up: float32 [768, 3072], P('batch')
- grad_up_bias: float32 [3072], P('batch')
- grad_down: float32 [3072, 768], P('batch')
- grad_down_bias: float32 [768], P('batch')
- grad_gain_two: float32 [768], P('batch')
- grad_shift_two: float32 [768], P('batch')
Inputs may be any that keep to these rules, and one draw needn't show every extreme that they name: `lengths`: in each group of 4 pages that one index of batch holds, at least one page has length 512. The 80 positions listed for a page are distinct; entries at or past the page's count are present but unused. `counts`: some page has exactly 80 masked positions.
All inputs are finite; a program needn't handle non-finite values.
Results may differ from a plain program's by a relative error of at most 0.02.
Values may be sent and summed in bfloat16 or wider, within the bound.
No kernel may reach another device: no remote copies, remote signals or barrier semaphores. Data moves between devices by JAX's collectives and lax.ppermute only.
A program may use at most 192 MiB of HBM per device.

v0:
```python
import jax
import jax.numpy as jnp
from jax import lax
from jax.sharding import PartitionSpec as P

HEADS = 12
HD = 64


SCALE = 0.125
NEGATIVE = -1e30
EPSILON = 1e-12


def shifted(shard, axis, by):
    peers = lax.axis_size(axis)
    return lax.ppermute(shard, axis, [(i, (i + by) % peers) for i in range(peers)])


def dot_plain(matrix_a, matrix_b):
    return jnp.dot(matrix_a, matrix_b, preferred_element_type=jnp.float32)


def dot_rows(matrix_a, matrix_b):
    return lax.dot_general(
        matrix_a, matrix_b, (((0,), (0,)), ((), ())), preferred_element_type=jnp.float32
    )


def dot_back(matrix_a, matrix_b):
    return lax.dot_general(
        matrix_a, matrix_b, (((1,), (1,)), ((), ())), preferred_element_type=jnp.float32
    )


def normed(values, gain, shift):
    centre = jnp.mean(values, axis=-1, keepdims=True)
    centred = values - centre
    spread = jnp.mean(centred * centred, axis=-1, keepdims=True)
    return centred * lax.rsqrt(spread + EPSILON) * gain + shift


def smooth(values):
    return jax.nn.gelu(values, approximate=False)


def place_rows(inputs, positions, counts, token_ids, table, offset):
    page_span = inputs.shape[1]
    slot_count = positions.shape[1]
    slot_live = jnp.arange(slot_count, dtype=jnp.int32)[None, :] < counts[:, None]
    local_spots = offset + jnp.arange(page_span, dtype=jnp.int32)
    slot_hits = (positions[:, :, None] == local_spots[None, None, :]) & slot_live[:, :, None]
    fetched = jnp.take(table, token_ids, axis=0)
    placed = jnp.einsum(
        "pms,pmd->psd", slot_hits.astype(jnp.bfloat16), fetched, preferred_element_type=jnp.float32
    ).astype(jnp.bfloat16)
    replaced = jnp.any(slot_hits, axis=1)
    return (jnp.where(replaced[..., None], placed, inputs), replaced)


def score_block(queries, key_part, key_start, lengths):
    key_count = key_part.shape[1]
    scores = (
        jnp.einsum("pshd,pnhd->phsn", queries, key_part, preferred_element_type=jnp.float32) * SCALE
    )
    key_spots = key_start + jnp.arange(key_count, dtype=jnp.int32)
    key_live = key_spots[None, :] < lengths[:, None]
    return (scores, key_live[:, None, None, :])


def merge_block(running, queries, key_part, value_part, key_start, lengths):
    row_max, weight_sum, summed = running
    scores, key_live = score_block(queries, key_part, key_start, lengths)
    masked = jnp.where(key_live, scores, NEGATIVE)
    new_max = jnp.maximum(row_max, jnp.max(masked, axis=-1))
    weights = jnp.where(key_live, jnp.exp(masked - new_max[..., None]), 0.0)
    weight_sum = jnp.sum(weights, axis=-1)
    summed = jnp.einsum(
        "phsn,pnhd->phsd",
        weights.astype(jnp.bfloat16),
        value_part,
        preferred_element_type=jnp.float32,
    )
    return (new_max, weight_sum, summed)


def key_grads(queries, d_summed, delta_row, row_max, lengths, key_part, value_part, key_start):
    scores, key_live = score_block(queries, key_part, key_start, lengths)
    masked = jnp.where(key_live, scores, NEGATIVE)
    weights = jnp.where(key_live, jnp.exp(masked - row_max[..., None]), 0.0)
    d_value_part = jnp.einsum(
        "phsn,phsd->pnhd",
        weights.astype(jnp.bfloat16),
        d_summed,
        preferred_element_type=jnp.float32,
    )
    d_prob = jnp.einsum("phsd,pnhd->phsn", d_summed, value_part, preferred_element_type=jnp.float32)
    d_scores = (weights * (d_prob - delta_row[..., None])).astype(jnp.bfloat16)
    d_query_part = jnp.einsum(
        "phsn,pnhd->pshd", d_scores, key_part, preferred_element_type=jnp.float32
    )
    d_key_part = jnp.einsum(
        "phsn,pshd->pnhd", d_scores, queries, preferred_element_type=jnp.float32
    )
    return (d_query_part, d_key_part, d_value_part)


def body(
    inputs,
    lengths,
    positions,
    counts,
    token_ids,
    table,
    w_query,
    b_query,
    w_key,
    w_value,
    b_value,
    w_out,
    b_out,
    gain_one,
    shift_one,
    w_up,
    b_up,
    w_down,
    b_down,
    gain_two,
    shift_two,
    cotangent,
):
    blocks_along = lax.axis_size("blk")
    own_index = lax.axis_index("blk")
    rows_work, back_work = (inputs, cotangent)
    lengths_work, positions_work, counts_work, names_work = (lengths, positions, counts, token_ids)
    first_spot = own_index * inputs.shape[1]
    page_count, page_span, model_width = rows_work.shape
    row_count = page_count * page_span
    start_rows, replaced = place_rows(
        rows_work, positions_work, counts_work, names_work, table, first_spot
    )
    flat_rows = start_rows.reshape(row_count, model_width)
    heads_shape = (page_count, page_span, HEADS, HD)
    queries = (dot_plain(flat_rows, w_query) + b_query).astype(jnp.bfloat16).reshape(heads_shape)
    keys_local = dot_plain(flat_rows, w_key).astype(jnp.bfloat16).reshape(heads_shape)
    values_local = (
        (dot_plain(flat_rows, w_value) + b_value).astype(jnp.bfloat16).reshape(heads_shape)
    )
    stat_shape = (page_count, HEADS, page_span)
    initial = (
        jnp.full(stat_shape, NEGATIVE, jnp.float32),
        jnp.zeros(stat_shape, jnp.float32),
        jnp.zeros((page_count, HEADS, page_span, HD), jnp.float32),
    )
    row_max, weight_sum, summed = merge_block(
        initial,
        queries,
        lax.all_gather(keys_local, "blk", axis=1, tiled=True),
        lax.all_gather(values_local, "blk", axis=1, tiled=True),
        jnp.int32(0),
        lengths_work,
    )
    mixed_heads = summed / weight_sum[..., None]
    attended = (
        mixed_heads.transpose(0, 2, 1, 3).reshape(row_count, model_width).astype(jnp.bfloat16)
    )
    branch = dot_plain(attended, w_out) + b_out
    resid_one = flat_rows.astype(jnp.float32) + branch
    normed_one, norm_one_back = jax.vjp(
        normed, resid_one, gain_one.astype(jnp.float32), shift_one.astype(jnp.float32)
    )
    normed_low = normed_one.astype(jnp.bfloat16)
    hidden = dot_plain(normed_low, w_up) + b_up
    activated, smooth_back = jax.vjp(smooth, hidden)
    active = activated.astype(jnp.bfloat16)
    down_out = dot_plain(active, w_down) + b_down
    final_rows, norm_two_back = jax.vjp(
        normed, normed_one + down_out, gain_two.astype(jnp.float32), shift_two.astype(jnp.float32)
    )
    outputs = final_rows.astype(jnp.bfloat16).reshape(rows_work.shape)
    d_resid_two, grad_gain_two, grad_shift_two = norm_two_back(
        back_work.reshape(row_count, model_width).astype(jnp.float32)
    )
    d_down = d_resid_two.astype(jnp.bfloat16)
    grad_down = dot_rows(active, d_down)
    grad_down_bias = jnp.sum(d_down, axis=0, dtype=jnp.float32)
    d_hidden = smooth_back(dot_back(d_down, w_down))[0].astype(jnp.bfloat16)
    grad_up = dot_rows(normed_low, d_hidden)
    grad_up_bias = jnp.sum(d_hidden, axis=0, dtype=jnp.float32)
    d_resid_one, grad_gain_one, grad_shift_one = norm_one_back(
        d_resid_two + dot_back(d_hidden, w_up)
    )
    d_branch = d_resid_one.astype(jnp.bfloat16)
    grad_out = dot_rows(attended, d_branch)
    grad_out_bias = jnp.sum(d_branch, axis=0, dtype=jnp.float32)
    d_mixed = dot_back(d_branch, w_out).reshape(heads_shape).transpose(0, 2, 1, 3)
    delta_row = jnp.sum(d_mixed * mixed_heads, axis=-1) / weight_sum
    d_summed = (d_mixed / weight_sum[..., None]).astype(jnp.bfloat16)

    def grads_for(key_part, value_part, key_start):
        return key_grads(
            queries, d_summed, delta_row, row_max, lengths_work, key_part, value_part, key_start
        )

    zero_heads = jnp.zeros(heads_shape, jnp.float32)

    def move_grads(grad_keys, grad_values):
        return (
            shifted(grad_keys.astype(jnp.bfloat16), "blk", 1).astype(grad_keys.dtype),
            shifted(grad_values.astype(jnp.bfloat16), "blk", 1).astype(grad_values.dtype),
        )

    def rotate_turn(turn_index, carried):
        key_part, value_part, key_run, value_run, query_run = carried
        owner_index = (own_index - turn_index) % blocks_along
        query_add, key_add, value_add = grads_for(key_part, value_part, owner_index * page_span)
        key_part, value_part = shifted((key_part, value_part), "blk", 1)
        key_run, value_run = move_grads(key_run + key_add, value_run + value_add)
        return (key_part, value_part, key_run, value_run, query_run + query_add)

    key_part, value_part, key_run, value_run, query_run = lax.fori_loop(
        0,
        blocks_along - 1,
        rotate_turn,
        (keys_local, values_local, zero_heads, zero_heads, zero_heads),
    )
    owner_index = (own_index + 1) % blocks_along
    query_add, key_add, value_add = grads_for(key_part, value_part, owner_index * page_span)
    d_queries = query_run + query_add
    d_keys, d_values = move_grads(key_run + key_add, value_run + value_add)
    d_query_rows = (d_queries * SCALE).astype(jnp.bfloat16).reshape(row_count, model_width)
    d_key_rows = (d_keys * SCALE).astype(jnp.bfloat16).reshape(row_count, model_width)
    d_value_rows = d_values.astype(jnp.bfloat16).reshape(row_count, model_width)
    grad_query = dot_rows(flat_rows, d_query_rows)
    grad_query_bias = jnp.sum(d_query_rows, axis=0, dtype=jnp.float32)
    grad_key = dot_rows(flat_rows, d_key_rows)
    grad_value = dot_rows(flat_rows, d_value_rows)
    grad_value_bias = jnp.sum(d_value_rows, axis=0, dtype=jnp.float32)
    d_start = (
        d_resid_one
        + dot_back(d_query_rows, w_query)
        + dot_back(d_key_rows, w_key)
        + dot_back(d_value_rows, w_value)
    )
    d_inputs = jnp.where(replaced[..., None], 0.0, d_start.reshape(rows_work.shape)).astype(
        jnp.bfloat16
    )
    (
        grad_query,
        grad_query_bias,
        grad_key,
        grad_value,
        grad_value_bias,
        grad_out,
        grad_out_bias,
        grad_gain_one,
        grad_shift_one,
        grad_up,
        grad_up_bias,
        grad_down,
        grad_down_bias,
        grad_gain_two,
        grad_shift_two,
    ) = (
        lax.psum_scatter(grad_query, "batch", scatter_dimension=0, tiled=True),
        lax.psum_scatter(grad_query_bias, "batch", scatter_dimension=0, tiled=True),
        lax.psum_scatter(grad_key, "batch", scatter_dimension=0, tiled=True),
        lax.psum_scatter(grad_value, "batch", scatter_dimension=0, tiled=True),
        lax.psum_scatter(grad_value_bias, "batch", scatter_dimension=0, tiled=True),
        lax.psum_scatter(grad_out, "batch", scatter_dimension=0, tiled=True),
        lax.psum_scatter(grad_out_bias, "batch", scatter_dimension=0, tiled=True),
        lax.psum_scatter(grad_gain_one, "batch", scatter_dimension=0, tiled=True),
        lax.psum_scatter(grad_shift_one, "batch", scatter_dimension=0, tiled=True),
        lax.psum_scatter(grad_up, "batch", scatter_dimension=0, tiled=True),
        lax.psum_scatter(grad_up_bias, "batch", scatter_dimension=0, tiled=True),
        lax.psum_scatter(grad_down, "batch", scatter_dimension=0, tiled=True),
        lax.psum_scatter(grad_down_bias, "batch", scatter_dimension=0, tiled=True),
        lax.psum_scatter(grad_gain_two, "batch", scatter_dimension=0, tiled=True),
        lax.psum_scatter(grad_shift_two, "batch", scatter_dimension=0, tiled=True),
    )
    (
        grad_query,
        grad_query_bias,
        grad_key,
        grad_value,
        grad_value_bias,
        grad_out,
        grad_out_bias,
        grad_gain_one,
        grad_shift_one,
        grad_up,
        grad_up_bias,
        grad_down,
        grad_down_bias,
        grad_gain_two,
        grad_shift_two,
    ) = (
        lax.psum(grad_query.astype(jnp.bfloat16), "blk").astype(jnp.float32),
        lax.psum(grad_query_bias.astype(jnp.bfloat16), "blk").astype(jnp.float32),
        lax.psum(grad_key.astype(jnp.bfloat16), "blk").astype(jnp.float32),
        lax.psum(grad_value.astype(jnp.bfloat16), "blk").astype(jnp.float32),
        lax.psum(grad_value_bias.astype(jnp.bfloat16), "blk").astype(jnp.float32),
        lax.psum(grad_out.astype(jnp.bfloat16), "blk").astype(jnp.float32),
        lax.psum(grad_out_bias.astype(jnp.bfloat16), "blk").astype(jnp.float32),
        lax.psum(grad_gain_one.astype(jnp.bfloat16), "blk").astype(jnp.float32),
        lax.psum(grad_shift_one.astype(jnp.bfloat16), "blk").astype(jnp.float32),
        lax.psum(grad_up.astype(jnp.bfloat16), "blk").astype(jnp.float32),
        lax.psum(grad_up_bias.astype(jnp.bfloat16), "blk").astype(jnp.float32),
        lax.psum(grad_down.astype(jnp.bfloat16), "blk").astype(jnp.float32),
        lax.psum(grad_down_bias.astype(jnp.bfloat16), "blk").astype(jnp.float32),
        lax.psum(grad_gain_two.astype(jnp.bfloat16), "blk").astype(jnp.float32),
        lax.psum(grad_shift_two.astype(jnp.bfloat16), "blk").astype(jnp.float32),
    )
    return (
        outputs,
        d_inputs,
        grad_query,
        grad_query_bias,
        grad_key,
        grad_value,
        grad_value_bias,
        grad_out,
        grad_out_bias,
        grad_gain_one,
        grad_shift_one,
        grad_up,
        grad_up_bias,
        grad_down,
        grad_down_bias,
        grad_gain_two,
        grad_shift_two,
    )


def solution(mesh):
    in_specs = (
        P("batch", "blk", None),
        P("batch"),
        P("batch", None),
        P("batch"),
        P("batch", None),
        P(),
        P(),
        P(),
        P(),
        P(),
        P(),
        P(),
        P(),
        P(),
        P(),
        P(),
        P(),
        P(),
        P(),
        P(),
        P(),
        P("batch", "blk", None),
    )
    out_specs = (
        P("batch", "blk", None),
        P("batch", "blk", None),
        P("batch", None),
        P("batch"),
        P("batch", None),
        P("batch", None),
        P("batch"),
        P("batch", None),
        P("batch"),
        P("batch"),
        P("batch"),
        P("batch", None),
        P("batch"),
        P("batch", None),
        P("batch"),
        P("batch"),
        P("batch"),
    )
    return jax.shard_map(body, mesh=mesh, in_specs=in_specs, out_specs=out_specs, check_vma=False)
```

profile of v0, /device:TPU:0, one launch (start us, length us, event | category | flops | bytes accessed | tf_op | source)
XLA Modules:
  0.0 830.8 jit_solution(1134034851118075097)
XLA Ops:
  9.0 13.2 %gather_fusion = bf16[320,768]{1,0:T(8,128)(2,1)S(1)} fusion(bf16[15360,768]{1,0:T(8,128)(2,1)} %param.29, s32[1024]{0:T(1024)S(1)} %pad_clamp_fusion), kind=kCustom, calls=%fused_computation | custom fusion | bytes 984320 | tf_op jit(solution)/shard_map/jit(_take)/gather | solution.py:53
  41.5 32.1 %all-gather.3.cloned.1.call-done = bf16[4,512,12,64]{1,3,2,0:T(8,128)(2,1)} async-done(((bf16[4,128,12,64]{1,3,2,0:T(8,128)(2,1)}), bf16[4,512,12,64]{1,3,2,0:T(8,128)(2,1)}) %all-gather.3.cloned.1.call-update) | async-done | bytes 3145744 | tf_op jit(solution)/shard_map/all_gather | solution.py:158
  77.9 4.5 copy-done.5
  86.3 33.0 %all-gather.5.cloned.1.call-done = bf16[4,512,12,64]{1,3,2,0:T(8,128)(2,1)} async-done(((bf16[4,128,12,64]{1,3,2,0:T(8,128)(2,1)}), bf16[4,512,12,64]{1,3,2,0:T(8,128)(2,1)}) %all-gather.5.cloned.1.call-update) | async-done | bytes 3145744 | tf_op jit(solution)/shard_map/all_gather | solution.py:159
  119.3 9.8 %fusion.40 = (bf16[4,128,12,64]{1,3,2,0:T(8,128)(2,1)S(1)}, f32[4,12,128,64]{2,3,1,0:T(8,128)}) fusion(f32[4,128,12]{1,2,0:T(8,128)S(1)} %bitcast.187, bf16[4,512,12,64]{1,3,2,0:T(8,128)(2,1)} %all-gather.5.cloned.1.call-done, f32[4,12,128,512]{3,2,1,0:T(8,128)} %copy-done.5, f32[4,12,128]{2,1,0:T(8,128)S(1)} %broadcast_maximum_fusion, ...), kind=kOutput, calls=%fused_computation.70 | convolution fusion | flops 419168256 | bytes 18139136 | tf_op jit(solution)/shard_map/phsn,pnhd->phsd/dot_general | solution.py:78
  131.2 20.1 %multiply_convert_fusion.1 = (bf16[512,3072]{1,0:T(8,128)(2,1)S(1)}, f32[512,3072]{1,0:T(8,128)}, f32[512,3072]{1,0:T(8,128)}) fusion(f32[3072]{0:T(1024)S(1)} %copy-done.43, bf16[768,3072]{1,0:T(8,128)(2,1)} %param.39, f32[512,768]{1,0:T(8,128)S(1)} %get-tuple-element.461, f32[768]{0:T(1024)S(1)} %copy-done.48, f32[768]{0:T(1024)S(1)} %convert_element_type.286, ...), kind=kOutput, calls=%fused_computation.29 | convolution fusion | flops 2521694208 | bytes 22042624 | tf_op jit(solution)/shard_map/dot_general | solution.py:21
  157.1 9.8 %convert_reduce_fusion = (f32[3072]{0:T(1024)}, bf16[512,3072]{1,0:T(8,128)(2,1)}) fusion(f32[512,3072]{1,0:T(8,128)} %get-tuple-element.452, f32[512,3072]{1,0:T(8,128)} %get-tuple-element.462, f32[3072]{0:T(1024)S(1)} %copy-done.43, bf16[512,768]{1,0:T(8,128)(2,1)S(1)} %get-tuple-element.442, bf16[3072,768]{1,0:T(8,128)(2,1)S(1)} %bitcast.189), kind=kOutput, calls=%fused_computation.27 | convolution fusion | flops 2442654720 | bytes 21258240 | tf_op jit(solution)/shard_map/dot_general | solution.py:31
  166.9 5.6 multiply_reduce_fusion
  183.1 238.8 %while.24 = (s32[]{:T(128)}, bf16[4,128,12,64]{1,3,2,0:T(8,128)(2,1)}, bf16[4,128,12,64]{1,3,2,0:T(8,128)(2,1)}, f32[4,128,12,64]{1,3,2,0:T(8,128)}, f32[4,128,1...) while((s32[]{:T(128)}, ...), condition=%wide.region_13.14_spmd.clone, body=%wide.region_12.13_spmd.clone.sunk | while | flops 516686464 | bytes 63777836 | solution.py:221
  202.6 11.7 %collective-permute-done.2 = bf16[4,128,12,64]{1,3,2,0:T(8,128)(2,1)} collective-permute-done((bf16[4,128,12,64]{1,3,2,0:T(8,128)(2,1)}, bf16[4,128,12,64]{1,3,2,0:T(8,128)(2,1)}, u32[]{:S(2)}, u32[]{:S(2)}) %collective-permute-start.2) | collective-permute-done | bytes 786464 | tf_op jit(solution)/shard_map/while/body/eval_jaxpr/ppermute | solution.py:17
  216.8 14.4 %collective-permute-done.3 = bf16[4,128,12,64]{1,3,2,0:T(8,128)(2,1)} collective-permute-done((bf16[4,128,12,64]{1,3,2,0:T(8,128)(2,1)}, bf16[4,128,12,64]{1,3,2,0:T(8,128)(2,1)}, u32[]{:S(2)}, u32[]{:S(2)}) %collective-permute-start.3) | collective-permute-done | bytes 786464 | tf_op jit(solution)/shard_map/while/body/eval_jaxpr/ppermute | solution.py:17
  233.7 14.4 %collective-permute-done = bf16[4,128,12,64]{1,3,2,0:T(8,128)(2,1)} collective-permute-done((bf16[4,128,12,64]{1,3,2,0:T(8,128)(2,1)S(1)}, bf16[4,128,12,64]{1,3,2,0:T(8,128)(2,1)}, u32[]{:S(2)}, u32[]{:S(2)}) %collective-permute-start) | collective-permute-done | bytes 786464 | tf_op jit(solution)/shard_map/while/body/eval_jaxpr/ppermute | solution.py:17
  248.1 15.7 %collective-permute-done.1 = bf16[4,128,12,64]{1,3,2,0:T(8,128)(2,1)} collective-permute-done((bf16[4,128,12,64]{1,3,2,0:T(8,128)(2,1)}, bf16[4,128,12,64]{1,3,2,0:T(8,128)(2,1)}, u32[]{:S(2)}, u32[]{:S(2)}) %collective-permute-start.1) | collective-permute-done | bytes 786464 | tf_op jit(solution)/shard_map/while/body/eval_jaxpr/ppermute | solution.py:17
  284.4 10.4 %collective-permute-done.2 = bf16[4,128,12,64]{1,3,2,0:T(8,128)(2,1)} collective-permute-done((bf16[4,128,12,64]{1,3,2,0:T(8,128)(2,1)}, bf16[4,128,12,64]{1,3,2,0:T(8,128)(2,1)}, u32[]{:S(2)}, u32[]{:S(2)}) %collective-permute-start.2) | collective-permute-done | bytes 786464 | tf_op jit(solution)/shard_map/while/body/eval_jaxpr/ppermute | solution.py:17
  297.3 14.4 %collective-permute-done.3 = bf16[4,128,12,64]{1,3,2,0:T(8,128)(2,1)} collective-permute-done((bf16[4,128,12,64]{1,3,2,0:T(8,128)(2,1)}, bf16[4,128,12,64]{1,3,2,0:T(8,128)(2,1)}, u32[]{:S(2)}, u32[]{:S(2)}) %collective-permute-start.3) | collective-permute-done | bytes 786464 | tf_op jit(solution)/shard_map/while/body/eval_jaxpr/ppermute | solution.py:17
  314.1 14.4 %collective-permute-done = bf16[4,128,12,64]{1,3,2,0:T(8,128)(2,1)} collective-permute-done((bf16[4,128,12,64]{1,3,2,0:T(8,128)(2,1)S(1)}, bf16[4,128,12,64]{1,3,2,0:T(8,128)(2,1)}, u32[]{:S(2)}, u32[]{:S(2)}) %collective-permute-start) | collective-permute-done | bytes 786464 | tf_op jit(solution)/shard_map/while/body/eval_jaxpr/ppermute | solution.py:17
  328.5 14.8 %collective-permute-done.1 = bf16[4,128,12,64]{1,3,2,0:T(8,128)(2,1)} collective-permute-done((bf16[4,128,12,64]{1,3,2,0:T(8,128)(2,1)}, bf16[4,128,12,64]{1,3,2,0:T(8,128)(2,1)}, u32[]{:S(2)}, u32[]{:S(2)}) %collective-permute-start.1) | collective-permute-done | bytes 786464 | tf_op jit(solution)/shard_map/while/body/eval_jaxpr/ppermute | solution.py:17
  364.0 10.4 %collective-permute-done.2 = bf16[4,128,12,64]{1,3,2,0:T(8,128)(2,1)} collective-permute-done((bf16[4,128,12,64]{1,3,2,0:T(8,128)(2,1)}, bf16[4,128,12,64]{1,3,2,0:T(8,128)(2,1)}, u32[]{:S(2)}, u32[]{:S(2)}) %collective-permute-start.2) | collective-permute-done | bytes 786464 | tf_op jit(solution)/shard_map/while/body/eval_jaxpr/ppermute | solution.py:17
  376.8 14.4 %collective-permute-done.3 = bf16[4,128,12,64]{1,3,2,0:T(8,128)(2,1)} collective-permute-done((bf16[4,128,12,64]{1,3,2,0:T(8,128)(2,1)}, bf16[4,128,12,64]{1,3,2,0:T(8,128)(2,1)}, u32[]{:S(2)}, u32[]{:S(2)}) %collective-permute-start.3) | collective-permute-done | bytes 786464 | tf_op jit(solution)/shard_map/while/body/eval_jaxpr/ppermute | solution.py:17
  393.6 14.4 %collective-permute-done = bf16[4,128,12,64]{1,3,2,0:T(8,128)(2,1)} collective-permute-done((bf16[4,128,12,64]{1,3,2,0:T(8,128)(2,1)S(1)}, bf16[4,128,12,64]{1,3,2,0:T(8,128)(2,1)}, u32[]{:S(2)}, u32[]{:S(2)}) %collective-permute-start) | collective-permute-done | bytes 786464 | tf_op jit(solution)/shard_map/while/body/eval_jaxpr/ppermute | solution.py:17
  408.0 13.8 %collective-permute-done.1 = bf16[4,128,12,64]{1,3,2,0:T(8,128)(2,1)} collective-permute-done((bf16[4,128,12,64]{1,3,2,0:T(8,128)(2,1)}, bf16[4,128,12,64]{1,3,2,0:T(8,128)(2,1)}, u32[]{:S(2)}, u32[]{:S(2)}) %collective-permute-start.1) | collective-permute-done | bytes 786464 | tf_op jit(solution)/shard_map/while/body/eval_jaxpr/ppermute | solution.py:17
  438.3 17.4 %collective-permute-done.5 = bf16[4,128,12,64]{1,3,2,0:T(8,128)(2,1)S(1)} collective-permute-done((bf16[4,128,12,64]{1,3,2,0:T(8,128)(2,1)S(1)}, bf16[4,128,12,64]{1,3,2,0:T(8,128)(2,1)S(1)}, u32[]{:S(2)}, u32[]{:S(2)}) %collective-permute-start.5) | collective-permute-done | bytes 786464 | tf_op jit(solution)/shard_map/ppermute | solution.py:17
  461.3 16.5 %collective-permute-done.4 = bf16[4,128,12,64]{1,3,2,0:T(8,128)(2,1)S(1)} collective-permute-done((bf16[4,128,12,64]{1,3,2,0:T(8,128)(2,1)S(1)}, bf16[4,128,12,64]{1,3,2,0:T(8,128)(2,1)S(1)}, u32[]{:S(2)}, u32[]{:S(2)}) %collective-permute-start.4) | collective-permute-done | bytes 786464 | tf_op jit(solution)/shard_map/ppermute | solution.py:17
  481.9 7.2 fusion.93
  490.2 8.2 fusion.104
  501.8 7.0 reduce-scatter.11.cloned.1.call-done
  510.5 36.1 %reduce-scatter.9.cloned.1.call-done = f32[96,768]{1,0:T(8,128)} async-done(((f32[768,768]{1,0:T(8,128)}), f32[96,768]{1,0:T(8,128)}) %reduce-scatter.9.cloned.1.call-update) | async-done | bytes 294928 | tf_op jit(solution)/shard_map/reduce_scatter | solution.py:267
  548.2 99.4 %reduce-scatter.15.cloned.1.call-done = f32[96,3072]{1,0:T(8,128)} async-done(((f32[768,3072]{1,0:T(8,128)}), f32[96,3072]{1,0:T(8,128)}) %reduce-scatter.15.cloned.1.call-update) | async-done | bytes 1179664 | tf_op jit(solution)/shard_map/reduce_scatter | solution.py:274
  649.7 98.0 %reduce-scatter.17.cloned.1.call-done = f32[384,768]{1,0:T(8,128)} async-done(((f32[3072,768]{1,0:T(8,128)}), f32[384,768]{1,0:T(8,128)}) %reduce-scatter.17.cloned.1.call-update) | async-done | bytes 1179664 | tf_op jit(solution)/shard_map/reduce_scatter | solution.py:276
  757.1 26.4 %all-reduce.9 = (bf16[768]{0:T(1024)(128)(2,1)S(1)}, bf16[768]{0:T(1024)(128)(2,1)S(1)}, bf16[768]{0:T(1024)(128)(2,1)S(1)}, bf16[768]{0:T(1024)(128)(2,1)S(1)},...) all-reduce(f32[768]{0:T(1024)S(1)} %reduce_sum.218, ...), channel_id=3, replica_groups=mesh['blk'=4,'batch'=8] {'batch'}, use_global_device_ids=true, to_apply=%region_17.18.clone | all-reduce | flops 9216 | bytes 55296
  784.2 10.0 %all-reduce.10 = (bf16[96]{0:T(256)(128)(2,1)S(1)}, bf16[96]{0:T(256)(128)(2,1)S(1)}, bf16[96]{0:T(256)(128)(2,1)S(1)}, bf16[96]{0:T(256)(128)(2,1)S(1)}, bf16[9...) all-reduce(bf16[96]{0:T(256)(128)(2,1)S(1)} %dynamic-slice.35, ...), channel_id=1, replica_groups=mesh['blk'=4,'batch'=8] {'blk'}, use_global_device_ids=true, to_apply=%region_18.19 | all-reduce | flops 1152 | bytes 4608 | tf_op jit(solution)/shard_map/psum | solution.py:299
  803.3 13.1 %all-reduce.14.cloned.1.call-done = (bf16[96,768]{1,0:T(8,128)(2,1)}, bf16[96,768]{1,0:T(8,128)(2,1)}, bf16[96,768]{1,0:T(8,128)(2,1)}, bf16[96,768]{1,0:T(8,128...) async-done(((bf16[96,768]{1,0:T(8,128)(2,1)}, bf16[96,768]{1,0:T(8,128)(2,1)}, bf16[96,768]{1,0:T(8,128)(2,1)}, bf16[96,768]{1,0:T(8,128)(2,1)}, ...) | async-done | bytes 1769488 | tf_op jit(solution)/shard_map/psum | solution.py:298
  (331 shorter events, 183.1 us)
Async XLA Ops:
  7.2 122.6 %copy-start = (bf16[768,768]{1,0:T(8,128)(2,1)S(1)}, bf16[768,768]{1,0:T(8,128)(2,1)}, u32[]{:S(2)}) copy-start(bf16[768,768]{1,0:T(8,128)(2,1)} %param.35) | copy-start | bytes 3538948
  7.2 66.4 %all-gather.3.cloned.1.call-start = ((), (), s32[]{:S(2)}) async-start(), calls=%async_computation.6 | async-start | bytes 3932160 | tf_op jit(solution)/shard_map/all_gather | solution.py:158
  23.0 106.8 %copy-start.12 = (bf16[4,128,768]{2,1,0:T(8,128)(2,1)}, bf16[4,128,768]{2,1,0:T(8,128)(2,1)S(1)}, u32[]{:S(2)}) copy-start(bf16[4,128,768]{2,1,0:T(8,128)(2,1)S(1)} %fusion.48) | copy-start | bytes 2359300
  26.9 92.4 %all-gather.5.cloned.1.call-start = ((), (), s32[]{:S(2)}) async-start(), calls=%async_computation.7 | async-start | bytes 3932160 | tf_op jit(solution)/shard_map/all_gather | solution.py:159
  30.6 467.9 %reduce-scatter.13.cloned.1.call-start = ((), (), s32[]{:S(2)}) async-start(), calls=%async_computation.11 | async-start | bytes 2654208 | tf_op jit(solution)/shard_map/reduce_scatter | solution.py:270
  33.5 44.3 %copy-start.6 = (bf16[4,128,12,64]{1,0,3,2:T(4,128)(2,1)}, bf16[4,128,12,64]{1,0,3,2:T(4,128)(2,1)S(1)}, u32[]{:S(2)}) copy-start(bf16[4,128,12,64]{1,0,3,2:T(4,128)(2,1)S(1)} %reshape.256) | copy-start | bytes 2359300
  34.8 116.5 %copy-start.40 = (f32[768]{0:T(1024)}, f32[768]{0:T(1024)S(1)}, u32[]{:S(2)}) copy-start(f32[768]{0:T(1024)S(1)} %convert_element_type.286) | copy-start | bytes 9220
  183.0 317.1 %reduce-scatter.7.cloned.1.call-start = ((), (), s32[]{:S(2)}) async-start(), calls=%async_computation.8 | async-start | bytes 2654208 | tf_op jit(solution)/shard_map/reduce_scatter | solution.py:265
  192.7 21.6 %collective-permute-start.2 = (bf16[4,128,12,64]{1,3,2,0:T(8,128)(2,1)}, bf16[4,128,12,64]{1,3,2,0:T(8,128)(2,1)}, u32[]{:S(2)}, u32[]{:S(2)}) collective-permute-start(bf16[4,128,12,64]{1,3,2,0:T(8,128)(2,1)} %fusion.173), channel_id=1, source_target_pairs={{0,8},{8,16},{16,24},{24,0},{1,9},{9,17},{17,25},{25,1},{2,10},{10... | collective-permute-start | bytes 2359304 | tf_op jit(solution)/shard_map/while/body/eval_jaxpr/ppermute | solution.py:17
  196.6 34.6 %collective-permute-start.3 = (bf16[4,128,12,64]{1,3,2,0:T(8,128)(2,1)}, bf16[4,128,12,64]{1,3,2,0:T(8,128)(2,1)}, u32[]{:S(2)}, u32[]{:S(2)}) collective-permute-start(bf16[4,128,12,64]{1,3,2,0:T(8,128)(2,1)} %fusion.174), channel_id=1, source_target_pairs={{0,8},{8,16},{16,24},{24,0},{1,9},{9,17},{17,25},{25,1},{2,10},{10... | collective-permute-start | bytes 2359304 | tf_op jit(solution)/shard_map/while/body/eval_jaxpr/ppermute | solution.py:17
  198.2 49.9 %collective-permute-start = (bf16[4,128,12,64]{1,3,2,0:T(8,128)(2,1)S(1)}, bf16[4,128,12,64]{1,3,2,0:T(8,128)(2,1)}, u32[]{:S(2)}, u32[]{:S(2)}) collective-permute-start(bf16[4,128,12,64]{1,3,2,0:T(8,128)(2,1)S(1)} %copy.137), channel_id=1, source_target_pairs={{0,8},{8,16},{16,24},{24,0},{1,9},{9,17},{17,25},{25,1},{2,10},{10... | collective-permute-start | bytes 2359304 | tf_op jit(solution)/shard_map/while/body/eval_jaxpr/ppermute | solution.py:17
  198.7 65.0 %collective-permute-start.1 = (bf16[4,128,12,64]{1,3,2,0:T(8,128)(2,1)}, bf16[4,128,12,64]{1,3,2,0:T(8,128)(2,1)}, u32[]{:S(2)}, u32[]{:S(2)}) collective-permute-start(bf16[4,128,12,64]{1,3,2,0:T(8,128)(2,1)} %copy.138), channel_id=1, source_target_pairs={{0,8},{8,16},{16,24},{24,0},{1,9},{9,17},{17,25},{25,1},{2,10},{10... | collective-permute-start | bytes 2359304 | tf_op jit(solution)/shard_map/while/body/eval_jaxpr/ppermute | solution.py:17
  273.1 21.7 %collective-permute-start.2 = (bf16[4,128,12,64]{1,3,2,0:T(8,128)(2,1)}, bf16[4,128,12,64]{1,3,2,0:T(8,128)(2,1)}, u32[]{:S(2)}, u32[]{:S(2)}) collective-permute-start(bf16[4,128,12,64]{1,3,2,0:T(8,128)(2,1)} %fusion.173), channel_id=1, source_target_pairs={{0,8},{8,16},{16,24},{24,0},{1,9},{9,17},{17,25},{25,1},{2,10},{10... | collective-permute-start | bytes 2359304 | tf_op jit(solution)/shard_map/while/body/eval_jaxpr/ppermute | solution.py:17
  276.2 35.5 %collective-permute-start.3 = (bf16[4,128,12,64]{1,3,2,0:T(8,128)(2,1)}, bf16[4,128,12,64]{1,3,2,0:T(8,128)(2,1)}, u32[]{:S(2)}, u32[]{:S(2)}) collective-permute-start(bf16[4,128,12,64]{1,3,2,0:T(8,128)(2,1)} %fusion.174), channel_id=1, source_target_pairs={{0,8},{8,16},{16,24},{24,0},{1,9},{9,17},{17,25},{25,1},{2,10},{10... | collective-permute-start | bytes 2359304 | tf_op jit(solution)/shard_map/while/body/eval_jaxpr/ppermute | solution.py:17
  278.6 49.9 %collective-permute-start = (bf16[4,128,12,64]{1,3,2,0:T(8,128)(2,1)S(1)}, bf16[4,128,12,64]{1,3,2,0:T(8,128)(2,1)}, u32[]{:S(2)}, u32[]{:S(2)}) collective-permute-start(bf16[4,128,12,64]{1,3,2,0:T(8,128)(2,1)S(1)} %copy.137), channel_id=1, source_target_pairs={{0,8},{8,16},{16,24},{24,0},{1,9},{9,17},{17,25},{25,1},{2,10},{10... | collective-permute-start | bytes 2359304 | tf_op jit(solution)/shard_map/while/body/eval_jaxpr/ppermute | solution.py:17
  278.6 64.6 %collective-permute-start.1 = (bf16[4,128,12,64]{1,3,2,0:T(8,128)(2,1)}, bf16[4,128,12,64]{1,3,2,0:T(8,128)(2,1)}, u32[]{:S(2)}, u32[]{:S(2)}) collective-permute-start(bf16[4,128,12,64]{1,3,2,0:T(8,128)(2,1)} %copy.138), channel_id=1, source_target_pairs={{0,8},{8,16},{16,24},{24,0},{1,9},{9,17},{17,25},{25,1},{2,10},{10... | collective-permute-start | bytes 2359304 | tf_op jit(solution)/shard_map/while/body/eval_jaxpr/ppermute | solution.py:17
  352.6 21.7 %collective-permute-start.2 = (bf16[4,128,12,64]{1,3,2,0:T(8,128)(2,1)}, bf16[4,128,12,64]{1,3,2,0:T(8,128)(2,1)}, u32[]{:S(2)}, u32[]{:S(2)}) collective-permute-start(bf16[4,128,12,64]{1,3,2,0:T(8,128)(2,1)} %fusion.173), channel_id=1, source_target_pairs={{0,8},{8,16},{16,24},{24,0},{1,9},{9,17},{17,25},{25,1},{2,10},{10... | collective-permute-start | bytes 2359304 | tf_op jit(solution)/shard_map/while/body/eval_jaxpr/ppermute | solution.py:17
  355.2 36.0 %collective-permute-start.3 = (bf16[4,128,12,64]{1,3,2,0:T(8,128)(2,1)}, bf16[4,128,12,64]{1,3,2,0:T(8,128)(2,1)}, u32[]{:S(2)}, u32[]{:S(2)}) collective-permute-start(bf16[4,128,12,64]{1,3,2,0:T(8,128)(2,1)} %fusion.174), channel_id=1, source_target_pairs={{0,8},{8,16},{16,24},{24,0},{1,9},{9,17},{17,25},{25,1},{2,10},{10... | collective-permute-start | bytes 2359304 | tf_op jit(solution)/shard_map/while/body/eval_jaxpr/ppermute | solution.py:17
  358.1 49.9 %collective-permute-start = (bf16[4,128,12,64]{1,3,2,0:T(8,128)(2,1)S(1)}, bf16[4,128,12,64]{1,3,2,0:T(8,128)(2,1)}, u32[]{:S(2)}, u32[]{:S(2)}) collective-permute-start(bf16[4,128,12,64]{1,3,2,0:T(8,128)(2,1)S(1)} %copy.137), channel_id=1, source_target_pairs={{0,8},{8,16},{16,24},{24,0},{1,9},{9,17},{17,25},{25,1},{2,10},{10... | collective-permute-start | bytes 2359304 | tf_op jit(solution)/shard_map/while/body/eval_jaxpr/ppermute | solution.py:17
  358.2 63.7 %collective-permute-start.1 = (bf16[4,128,12,64]{1,3,2,0:T(8,128)(2,1)}, bf16[4,128,12,64]{1,3,2,0:T(8,128)(2,1)}, u32[]{:S(2)}, u32[]{:S(2)}) collective-permute-start(bf16[4,128,12,64]{1,3,2,0:T(8,128)(2,1)} %copy.138), channel_id=1, source_target_pairs={{0,8},{8,16},{16,24},{24,0},{1,9},{9,17},{17,25},{25,1},{2,10},{10... | collective-permute-start | bytes 2359304 | tf_op jit(solution)/shard_map/while/body/eval_jaxpr/ppermute | solution.py:17
  434.7 74.2 %reduce-scatter.11.cloned.1.call-start = ((), (), s32[]{:S(2)}) async-start(), calls=%async_computation.10 | async-start | bytes 2654208 | tf_op jit(solution)/shard_map/reduce_scatter | solution.py:268
  438.3 17.5 %collective-permute-start.5 = (bf16[4,128,12,64]{1,3,2,0:T(8,128)(2,1)S(1)}, bf16[4,128,12,64]{1,3,2,0:T(8,128)(2,1)S(1)}, u32[]{:S(2)}, u32[]{:S(2)}) collective-permute-start(bf16[4,128,12,64]{1,3,2,0:T(8,128)(2,1)S(1)} %fusion.30), channel_id=1, source_target_pairs={{0,8},{8,16},{16,24},{24,0},{1,9},{9,17},{17,25},{25,1},{2,10},{10... | collective-permute-start | bytes 2359304 | tf_op jit(solution)/shard_map/ppermute | solution.py:17
  458.9 87.6 %reduce-scatter.9.cloned.1.call-start = ((), (), s32[]{:S(2)}) async-start(), calls=%async_computation.9 | async-start | bytes 2654208 | tf_op jit(solution)/shard_map/reduce_scatter | solution.py:267
  461.0 16.8 %collective-permute-start.4 = (bf16[4,128,12,64]{1,3,2,0:T(8,128)(2,1)S(1)}, bf16[4,128,12,64]{1,3,2,0:T(8,128)(2,1)S(1)}, u32[]{:S(2)}, u32[]{:S(2)}) collective-permute-start(bf16[4,128,12,64]{1,3,2,0:T(8,128)(2,1)S(1)} %fusion.31), channel_id=1, source_target_pairs={{0,8},{8,16},{16,24},{24,0},{1,9},{9,17},{17,25},{25,1},{2,10},{10... | collective-permute-start | bytes 2359304 | tf_op jit(solution)/shard_map/ppermute | solution.py:17
  481.8 165.8 %reduce-scatter.15.cloned.1.call-start = ((), (), s32[]{:S(2)}) async-start(), calls=%async_computation.12 | async-start | bytes 10616832 | tf_op jit(solution)/shard_map/reduce_scatter | solution.py:274
  489.1 258.6 %reduce-scatter.17.cloned.1.call-start = ((), (), s32[]{:S(2)}) async-start(), calls=%async_computation.13 | async-start | bytes 10616832 | tf_op jit(solution)/shard_map/reduce_scatter | solution.py:276
  498.4 318.0 %all-reduce.14.cloned.1.call-start = ((), (), s32[]{:S(2)}) async-start(), calls=%async_computation.14 | async-start | bytes 3538944 | tf_op jit(solution)/shard_map/psum | solution.py:298
  548.2 201.8 %copy-start.63 = (u32[32]{0:T(128)S(1)}, u32[32]{0:T(128)}, u32[]{:S(2)}) copy-start(u32[32]{0:T(128)} %constant.211) | copy-start | bytes 388
  548.2 203.7 %copy-start.11 = (bf16[4,128,768]{2,1,0:T(8,128)(2,1)S(1)}, bf16[4,128,768]{2,1,0:T(8,128)(2,1)}, u32[]{:S(2)}) copy-start(bf16[4,128,768]{2,1,0:T(8,128)(2,1)} %param.45) | copy-start | bytes 2359300
  649.7 102.4 %copy-start.24 = (bf16[4,128,12,64]{1,0,3,2:T(4,128)(2,1)S(1)}, bf16[4,128,12,64]{1,0,3,2:T(4,128)(2,1)}, u32[]{:S(2)}) copy-start(bf16[4,128,12,64]{1,0,3,2:T(4,128)(2,1)} %copy-done.23) | copy-start | bytes 2359300
  752.1 46.9 %copy-start.22 = (bf16[4,128,12,64]{1,0,3,2:T(4,128)(2,1)S(1)}, bf16[4,128,12,64]{1,0,3,2:T(4,128)(2,1)}, u32[]{:S(2)}) copy-start(bf16[4,128,12,64]{1,0,3,2:T(4,128)(2,1)} %copy-done.21) | copy-start | bytes 2359300
  755.5 45.6 %copy-start.9 = (f32[512,768]{1,0:T(8,128)S(1)}, f32[512,768]{1,0:T(8,128)}, u32[]{:S(2)}) copy-start(f32[512,768]{1,0:T(8,128)} %copy-done.8) | copy-start | bytes 4718596
  (67 other events, 504.6 us)
Sparse Core Ops, SparseCore 0:
  27.0 46.5 all-gather.2
  75.4 43.8 all-gather.4
  183.1 36.3 reduce-scatter.12
  434.8 36.3 reduce-scatter.6
  473.3 35.4 reduce-scatter.10
  511.0 35.5 reduce-scatter.8
  548.9 98.6 reduce-scatter.14
  649.9 97.8 reduce-scatter.16
  752.7 63.6 all-reduce.13
where the time goes:
time: 841 us; the launch traced here: 831 us
  waiting for transfers between devices  516 us (61%)
  matrix products  142 us (17%)
  other arithmetic  62.1 us (7%)
  local copies, waits for them, and re-layouts  41.8 us (5%)
  blocking collectives  36.4 us (4%)
  between operations  16.7 us (2%)
  starting transfers between devices  15.6 us (2%)
    ppermute x14, waiting for transfers between devices, shifted(): lax.ppermute(shard, axis, [(i, (i + by) % peers) for i in range(peers)])  197 us
    reduce_scatter x1, waiting for transfers between devices, body(): lax.psum_scatter(grad_up, 'batch', scatter_dimension=0, tiled=True)  99.4 us
    reduce_scatter x1, waiting for transfers between devices, body(): lax.psum_scatter(grad_down, 'batch', scatter_dimension=0, tiled=True)  98 us
    reduce_scatter x1, waiting for transfers between devices, body(): lax.psum_scatter(grad_key, 'batch', scatter_dimension=0, tiled=True)  36.1 us
    all_gather x1, waiting for transfers between devices, body(): lax.all_gather(values_local, 'blk', axis=1, tiled=True)  33 us
    all_gather x1, waiting for transfers between devices, body(): lax.all_gather(keys_local, 'blk', axis=1, tiled=True)  32.1 us
    dot_general x6, matrix products, dot_plain(): return jnp.dot(matrix_a, matrix_b, preferred_element_type=jnp.float32)  30.3 us
    unnamed x1, blocking collectives  26.4 us
  transfers between devices with their start and end apart: 23, of which 21 were waited for; matrix products, arithmetic and copies ran while one was open for 17% of the time, Pallas kernels for 0%

commit v1 on v0

v1 whole, which is shorter than its diff:
```python
import functools

import jax
import jax.numpy as jnp
from jax import lax
from jax.experimental import pallas as pl
from jax.experimental.pallas import tpu as pltpu
from jax.sharding import PartitionSpec as P

HEADS = 12
HD = 64
SCALE = 0.125
NEGATIVE = -1e30
EPSILON = 1e-12
BF = jnp.bfloat16
F32 = jnp.float32
MIB = 1024 * 1024


def nn(a, b):
    return lax.dot_general(a, b, (((1,), (0,)), ((), ())), preferred_element_type=F32)


def nt(a, b):
    return lax.dot_general(a, b, (((1,), (1,)), ((), ())), preferred_element_type=F32)


def tn(a, b):
    return lax.dot_general(a, b, (((0,), (0,)), ((), ())), preferred_element_type=F32)


def head_lanes(shape, which):
    lane = lax.broadcasted_iota(jnp.int32, shape, 1)
    return (lane >= HD) if which else (lane < HD)


def hits_of(pos_ref, count, rows, slots):
    spot = lax.broadcasted_iota(jnp.int32, (rows, slots), 0)
    slot = lax.broadcasted_iota(jnp.int32, (rows, slots), 1)
    return (pos_ref[...] == spot) & (slot < count)


def norm_parts(v):
    width = v.shape[-1]
    centre = jnp.sum(v, axis=-1, keepdims=True) * (1.0 / width)
    centred = v - centre
    spread = jnp.sum(centred * centred, axis=-1, keepdims=True) * (1.0 / width)
    rstd = lax.rsqrt(spread + EPSILON)
    return centred * rstd, rstd


def norm_back(c2, n, rstd):
    width = c2.shape[-1]
    a = jnp.sum(c2, axis=-1, keepdims=True) * (1.0 / width)
    b = jnp.sum(c2 * n, axis=-1, keepdims=True) * (1.0 / width)
    return (c2 - a - n * b) * rstd


def colsum(v):
    return jnp.sum(v, axis=0, keepdims=True)


def attend_kernel(
    info_ref, own_ref, p1_ref, p2_ref, p3_ref, pos_ref, fetched_ref,
    wq_ref, bq_ref, wk_ref, wv_ref, bv_ref, wo_ref, bo_ref,
    x_ref, q_ref, k_ref, v_ref, att_ref, max_ref, sum_ref, n_ref, rstd_ref,
    work_ref, att_rows,
):
    length, count, me = info_ref[0], info_ref[1], info_ref[2]
    rows, width = x_ref.shape
    span = own_ref.shape[0]
    for step, piece in enumerate((own_ref, p1_ref, p2_ref, p3_ref)):
        at = pl.multiple_of((me ^ step) * span, span)
        work_ref[pl.ds(at, span), :] = piece[...]
    hits = hits_of(pos_ref, count, rows, pos_ref.shape[1])
    onehot = hits.astype(F32)
    replaced = jnp.sum(onehot, axis=1, keepdims=True) > 0.5
    placed = nn(onehot.astype(BF), fetched_ref[...]).astype(BF)
    x = jnp.where(replaced, placed, work_ref[...])
    x_ref[...] = x
    q_ref[...] = ((nn(x, wq_ref[...]) + bq_ref[...]).astype(BF).astype(F32) * SCALE).astype(BF)
    k_ref[...] = nn(x, wk_ref[...]).astype(BF)
    v_ref[...] = (nn(x, wv_ref[...]) + bv_ref[...]).astype(BF)
    dead = jnp.where(lax.broadcasted_iota(jnp.int32, (rows, 1), 0) < length, 0.0, NEGATIVE)

    def pair(i, carry):
        lanes = pl.ds(pl.multiple_of(i * 2 * HD, 2 * HD), 2 * HD)
        q2, k2 = q_ref[:, lanes], k_ref[:, lanes]
        v2t = v_ref[:, lanes].T
        for h in range(2):
            qm = jnp.where(head_lanes(q2.shape, h), q2, jnp.zeros_like(q2))
            s = nt(k2, qm) + dead
            top = jnp.max(s, axis=0, keepdims=True)
            p = jnp.exp(s - top)
            total = jnp.sum(p, axis=0, keepdims=True)
            o = nn(v2t[h * HD:(h + 1) * HD], p.astype(BF)) / total
            max_ref[2 * i + h] = top
            sum_ref[2 * i + h] = total
            att_ref[pl.ds(pl.multiple_of(i * 2 * HD + h * HD, HD), HD), :] = o.astype(BF)
        att_rows[:, lanes] = att_ref[pl.ds(pl.multiple_of(i * 2 * HD, 2 * HD), 2 * HD), :].T
        return carry

    lax.fori_loop(0, HEADS // 2, pair, 0)
    branch = nn(att_rows[...], wo_ref[...]) + bo_ref[...]
    n, rstd = norm_parts(x_ref[...].astype(F32) + branch)
    n_ref[...] = n
    rstd_ref[...] = jnp.broadcast_to(rstd, rstd_ref.shape)


def gelu_both(v):
    e = jnp.exp(v * v * -0.5)
    t = 1.0 / (1.0 + 0.3275911 * 0.7071067811865476 * jnp.abs(v))
    poly = t * (0.5 * 0.254829592 + t * (0.5 * -0.284496736 + t * (0.5 * 1.421413741 + t * (0.5 * -1.453152027 + t * (0.5 * 1.061405429)))))
    tail = poly * e
    phi = jnp.where(v >= 0, 1.0 - tail, tail)
    return v * phi, phi + v * (e * 0.3989422804014327)


def ff_kernel(
    packed, shares, info_ref, n_ref, rstd_ref, att_ref, sum_ref,
    c0_ref, c1_ref, c2_ref, c3_ref,
    wu_ref, bu_ref, wd_ref, bd_ref, wo_ref, g1_ref, s1_ref, g2_ref, s2_ref,
    out_ref, gdu_ref, go_ref, dr_ref, dst_ref, delta_ref,
    bd_out, bu_out, bo_out, gg1_ref, gs1_ref, gg2_ref, gs2_ref,
    act, slope, dh, cot, nlow, nlow_t, dd, dfirst,
):
    rows, width = n_ref.shape
    ff = wu_ref.shape[1]
    step = 512
    span = c0_ref.shape[0]
    me, core = info_ref[2], info_ref[3]
    for hop, piece in enumerate((c0_ref, c1_ref, c2_ref, c3_ref)):
        at = pl.multiple_of((me ^ hop) * span, span)
        cot[pl.ds(at, span), :] = piece[...]
    normed = n_ref[...] * g1_ref[...] + s1_ref[...]
    nlow[...] = normed.astype(BF)
    nlow_t[...] = nlow[...].T

    def up(i, carry):
        lanes = pl.ds(pl.multiple_of(i * step, step), step)
        h = nn(nlow[...], wu_ref[:, lanes]) + bu_ref[:, lanes]
        a, b = gelu_both(h)
        act[:, lanes] = a.astype(BF)
        slope[:, lanes] = b.astype(BF)
        return carry

    lax.fori_loop(0, ff // step, up, 0)
    resid = n_ref[...] * g1_ref[...] + s1_ref[...] + nn(act[...], wd_ref[...]) + bd_ref[...]
    n2, rstd2 = norm_parts(resid)
    out_ref[...] = (n2 * g2_ref[...] + s2_ref[...]).astype(BF)
    c = cot[...].astype(F32)
    gg2_ref[...] = colsum(c * n2)
    gs2_ref[...] = colsum(c)
    d_r2 = norm_back(c * g2_ref[...], n2, rstd2)
    dfirst[...] = d_r2
    dd[...] = d_r2.astype(BF)
    bd_out[...] = colsum(dd[...].astype(F32))

    def back(i, carry):
        lanes = pl.ds(pl.multiple_of(i * width, width), width)
        g_down = tn(act[:, lanes], dd[...]).astype(BF)
        dhc = (nt(dd[...], wd_ref[lanes, :]) * slope[:, lanes].astype(F32)).astype(BF)
        dh[:, lanes] = dhc
        bu_out[:, lanes] = colsum(dhc.astype(F32))
        g_up = nn(nlow_t[...], dhc).astype(BF)
        if packed:
            unit = width // shares
            for c in range(2):
                for p in range(4):
                    at = (c * 4 + p) * unit
                    gdu_ref[c ^ core, p, i, 0] = g_down[at:at + unit]
                for z in range(shares // 2):
                    at = (2 * z + c) * unit
                    gdu_ref[c ^ core, i, z, 1] = g_up[at:at + unit]
        else:
            gdu_ref[0, lanes, :] = g_down
            gdu_ref[1, lanes, :] = g_up
        return carry

    lax.fori_loop(0, ff // width, back, 0)
    d_f = dfirst[...] + nt(dh[...], wu_ref[...])
    n1 = n_ref[...]
    gg1_ref[...] = colsum(d_f * n1)
    gs1_ref[...] = colsum(d_f)
    d_r1 = norm_back(d_f * g1_ref[...], n1, rstd_ref[:, 0:1])
    dr_ref[...] = d_r1
    db = d_r1.astype(BF)
    dd[...] = db
    bo_out[...] = colsum(db.astype(F32))
    go_ref[...] = nn(att_ref[...], dd[...]).astype(BF)
    for i in range(HEADS):
        at = slice(i * HD, (i + 1) * HD)
        dm = nt(wo_ref[at, :], dd[...])
        inv = 1.0 / sum_ref[i]
        delta_ref[i] = colsum(dm * att_ref[at, :].astype(F32)) * inv
        dst_ref[at, :] = (dm * inv).astype(BF)


def back_kernel(
    packed, shares, info_ref, pos_ref, x_ref, q_ref, k_ref, v_ref, dst_ref, delta_ref, max_ref, dr_ref, go_ref,
    wq_ref, wk_ref, wv_ref,
    ga_ref, bq_out, bv_out, din_ref,
    x_t, dq, dk, dv,
):
    length, count = info_ref[0], info_ref[1]
    rows, width = x_ref.shape
    x_t[...] = x_ref[...].T
    dead = jnp.where(lax.broadcasted_iota(jnp.int32, (rows, 1), 0) < length, 0.0, NEGATIVE)

    def pair(i, carry):
        at = pl.multiple_of(i * 2 * HD, 2 * HD)
        lanes = pl.ds(at, 2 * HD)
        q2, k2, v2 = q_ref[:, lanes], k_ref[:, lanes], v_ref[:, lanes]
        dst = dst_ref[pl.ds(at, 2 * HD), :]
        ds2 = dst.T
        k2t = k2.T
        dv2 = jnp.zeros((rows, 2 * HD), F32)
        dk2 = jnp.zeros((rows, 2 * HD), F32)
        dqs = []
        for h in range(2):
            live = head_lanes(q2.shape, h)
            zero = jnp.zeros_like(q2)
            qm = jnp.where(live, q2, zero)
            s = nt(k2, qm) + dead
            p = jnp.exp(s - max_ref[2 * i + h])
            dp = nn(jnp.where(live, v2, zero), dst)
            dsc = (p * (dp - delta_ref[2 * i + h])).astype(BF)
            dv2 = dv2 + nn(p.astype(BF), jnp.where(live, ds2, zero))
            dk2 = dk2 + nn(dsc, qm)
            dqs.append(nn(k2t[h * HD:(h + 1) * HD], dsc))
        dq[:, lanes] = (jnp.concatenate(dqs, axis=0) * SCALE).astype(BF).T
        dk[:, lanes] = dk2.astype(BF)
        dv[:, lanes] = dv2.astype(BF)
        return carry

    lax.fori_loop(0, HEADS // 2, pair, 0)
    bq_out[...] = colsum(dq[...].astype(F32))
    bv_out[...] = colsum(dv[...].astype(F32))
    core = info_ref[3]
    for i, part in enumerate((dq, dk, dv, None)):
        g = go_ref[...] if part is None else nn(x_t[...], part[...]).astype(BF)
        if packed:
            unit = width // shares
            for b in range(shares):
                ga_ref[(b % 2) ^ core, i, b // 2] = g[b * unit:(b + 1) * unit]
        else:
            ga_ref[i] = g
    total = dr_ref[...] + nt(dq[...], wq_ref[...]) + nt(dk[...], wk_ref[...]) + nt(dv[...], wv_ref[...])
    hits = hits_of(pos_ref, count, rows, pos_ref.shape[1]).astype(F32)
    replaced = jnp.sum(hits, axis=1, keepdims=True) > 0.5
    din_ref[...] = jnp.where(replaced, 0.0, total).astype(BF)


VM = pl.BlockSpec(memory_space=pltpu.VMEM)
SM = pl.BlockSpec(memory_space=pltpu.SMEM)


def call(kernel, args, outs, scratch, flops):
    moved = sum(a.size * a.dtype.itemsize for a in args)
    return pl.pallas_call(
        kernel,
        out_shape=[jax.ShapeDtypeStruct(s, d) for s, d in outs],
        in_specs=[SM] + [VM] * (len(args) - 1),
        out_specs=[VM] * len(outs),
        scratch_shapes=[pltpu.VMEM(s, d) for s, d in scratch],
        compiler_params=pltpu.CompilerParams(vmem_limit_bytes=60 * MIB),
        cost_estimate=pl.CostEstimate(flops=flops, bytes_accessed=moved, transcendentals=0),
    )(*args)


def attend(info, pieces, pos, fetched, wq, bq, wk, wv, bv, wo, bo):
    span, width = pieces[0].shape
    rows = 4 * span
    args = (info, *pieces, pos, fetched, wq, bq, wk, wv, bv, wo, bo)
    outs = [((rows, width), BF)] * 4 + [((width, rows), BF), ((HEADS, 1, rows), F32), ((HEADS, 1, rows), F32), ((rows, width), F32), ((rows, 128), F32)]
    flops = 8 * rows * width * width + 4 * rows * rows * width * 4
    return call(attend_kernel, args, outs, [((rows, width), BF)] * 2, flops)


def feed(packed, shares, info, n, rstd, att, sums, pieces, wu, bu, wd, bd, wo, g1, s1, g2, s2):
    rows, width = n.shape
    ff = wu.shape[1]
    args = (info, n, rstd, att, sums, *pieces, wu, bu, wd, bd, wo, g1, s1, g2, s2)
    gdu = (2, 4, shares // 2, 2, width // shares, width) if packed else (2, ff, width)
    outs = [((rows, width), BF), (gdu, BF), ((width, width), BF), ((rows, width), F32), ((width, rows), BF), ((HEADS, 1, rows), F32)]
    outs += [((1, width), F32), ((1, ff), F32)] + [((1, width), F32)] * 5
    scratch = [((rows, ff), BF)] * 3 + [((rows, width), BF)] * 2 + [((width, rows), BF), ((rows, width), BF), ((rows, width), F32)]
    flops = 12 * rows * width * ff + 4 * rows * width * width
    return call(functools.partial(ff_kernel, packed, shares), args, outs, scratch, flops)


def back(packed, shares, info, pos, x, q, k, v, dst, delta, tops, dr, go, wq, wk, wv):
    rows, width = x.shape
    args = (info, pos, x, q, k, v, dst, delta, tops, dr, go, wq, wk, wv)
    ga = (2, 4, shares // 2, width // shares, width) if packed else (4, width, width)
    outs = [(ga, BF)] + [((1, width), F32)] * 2 + [((rows, width), BF)]
    scratch = [((width, rows), BF)] + [((rows, width), BF)] * 3
    flops = 12 * rows * width * width + 10 * rows * rows * width * 4
    return call(functools.partial(back_kernel, packed, shares), args, outs, scratch, flops)


def pick(array, index):
    return lax.dynamic_index_in_dim(array, index, 0, keepdims=False)


def swap(array, bit):
    return lax.ppermute(array, "blk", [(i, i ^ bit) for i in range(lax.axis_size("blk"))])


def swap_first(array, first):
    blks, shares = lax.axis_size("blk"), lax.axis_size("batch")
    perm = []
    for b in range(blks):
        for s in range(shares):
            bit = 1 if (s % 2 == 0) == first else 2
            perm.append((b * shares + s, (b ^ bit) * shares + s))
    return lax.ppermute(array, ("blk", "batch"), perm)


def swap_batch(array, bit):
    return lax.ppermute(array, "batch", [(i, i ^ bit) for i in range(lax.axis_size("batch"))])


def added(a, b):
    return (a.astype(F32) + b.astype(F32)).astype(BF)


def halve(data, mine, move):
    return added(pick(data, mine), move(pick(data, 1 - mine)))


def joined(own, other, mine):
    return jnp.where(mine == 0, jnp.stack([own, other]), jnp.stack([other, own]))


def reduce_all(packed, where):
    blk, share, core = where
    shares = lax.axis_size("batch")
    x_bit, y_bit = blk % 2, blk // 2
    hi = jnp.where(core == 0, x_bit, y_bit)
    lo = jnp.where(core == 0, y_bit, x_bit)
    data = added(packed[0], swap_batch(packed[1], 1))
    data = halve(data.reshape((2, 2) + data.shape[1:]), hi, lambda v: swap_first(v, True))
    data = halve(data, lo, lambda v: swap_first(v, False))
    bit = 2
    while bit < shares:
        data = data.reshape((data.shape[0] // 2, 2) + data.shape[1:])
        mine = (share // bit) % 2
        data = added(
            lax.dynamic_index_in_dim(data, mine, 1, keepdims=False),
            swap_batch(lax.dynamic_index_in_dim(data, 1 - mine, 1, keepdims=False), bit),
        )
        bit *= 2
    data = data[0]
    data = joined(data, swap_first(data, False), lo)
    data = joined(data, swap_first(data, True), hi)
    return data.reshape((4,) + data.shape[2:])


def body(
    inputs, lengths, positions, counts, token_ids, table,
    w_query, b_query, w_key, w_value, b_value, w_out, b_out, gain_one, shift_one,
    w_up, b_up, w_down, b_down, gain_two, shift_two, cotangent,
):
    blk, share = lax.axis_index("blk"), lax.axis_index("batch")
    shares = lax.axis_size("batch")
    core = share % 2
    where = (blk, share, core)
    pages, span, width = inputs.shape
    ff = w_up.shape[1]
    unit = width // shares
    packed = shares == 8
    info = jnp.stack([pick(lengths, blk), pick(counts, blk), blk, core]).astype(jnp.int32)
    rows_in = [pick(inputs, blk)] + [swap(pick(inputs, blk ^ i), i) for i in range(1, pages)]
    back_in = [pick(cotangent, blk)] + [swap(pick(cotangent, blk ^ i), i) for i in range(1, pages)]
    slots = positions.shape[1]
    pos = jnp.pad(pick(positions, blk), (0, 128 - slots), constant_values=-1).reshape(1, 128)
    fetched = jnp.take(table, jnp.pad(pick(token_ids, blk), (0, 128 - slots)), axis=0)

    def row(v):
        return v.astype(F32).reshape(1, -1)

    x, q, k, v, att, tops, sums, n1, rstd = attend(
        info, rows_in, pos, fetched, w_query, row(b_query), w_key, w_value, row(b_value), w_out, row(b_out)
    )
    (out_page, gdu, g_out, d_r1, dst, delta, v_down, v_up, v_out, v_gain1, v_shift1, v_gain2, v_shift2) = feed(
        packed, shares, info, n1, rstd, att, sums, back_in, w_up, row(b_up), w_down, row(b_down), w_out,
        row(gain_one), row(shift_one), row(gain_two), row(shift_two),
    )
    ga, v_query, v_value, d_page = back(
        packed, shares, info, pos, x, q, k, v, dst, delta, tops, d_r1, g_out, w_query, w_key, w_value
    )

    def to_pages(page):
        parts = page.reshape(pages, span, width)
        result = jnp.zeros_like(parts)
        for i in range(pages):
            part = pick(parts, blk ^ i)
            part = part if i == 0 else swap(part, i)
            result = lax.dynamic_update_index_in_dim(result, part, blk ^ i, 0)
        return result

    outputs = to_pages(out_page)
    d_inputs = to_pages(d_page)
    if not packed:
        down = gdu[0].reshape(shares // 2, 2, 4, unit, width).transpose(1, 2, 0, 3, 4)
        up = gdu[1].reshape(4, shares // 2, 2, unit, width).transpose(2, 0, 1, 3, 4)
        gdu = jnp.stack([down, up], axis=3)
        ga = ga.reshape(4, shares // 2, 2, unit, width).transpose(2, 0, 1, 3, 4)
        gdu = jnp.where(core == 0, gdu, gdu[::-1])
        ga = jnp.where(core == 0, ga, ga[::-1])
    du = reduce_all(gdu, where).astype(F32)
    grads = reduce_all(ga, where).astype(F32)
    grad_down = du[:, 0].reshape(ff // shares, width)
    grad_up = du[:, 1].transpose(1, 0, 2).reshape(unit, ff)
    grad_query, grad_key, grad_value, grad_out = (grads[i] for i in range(4))
    vectors = [v_query, v_value, v_out, v_gain1, v_shift1, v_up, v_down, v_gain2, v_shift2]
    stacked = jnp.concatenate([u.reshape(shares, -1) for u in vectors], axis=1)
    mine = pick(lax.psum(stacked, ("blk", "batch")), share)
    sizes = [u.size // shares for u in vectors]
    cuts = [sum(sizes[:i]) for i in range(len(sizes) + 1)]
    r = [mine[cuts[i]:cuts[i + 1]] for i in range(len(sizes))]
    return (
        outputs, d_inputs, grad_query, r[0], grad_key, grad_value, r[1], grad_out, r[2],
        r[3], r[4], grad_up, r[5], grad_down, r[6], r[7], r[8],
    )


def solution(mesh):
    split, whole = P("batch", "blk", None), P()
    rows, vec = P("batch", None), P("batch")
    in_specs = (split, vec, rows, vec, rows) + (whole,) * 16 + (split,)
    out_specs = (split, split, rows, vec, rows, rows, vec, rows, vec, vec, vec, rows, vec, rows, vec, vec, vec)
    return jax.shard_map(body, mesh=mesh, in_specs=in_specs, out_specs=out_specs, check_vma=False)
```

time: 841 us -> 304 us (0.36); the launches traced: 831 us -> 303 us
  waiting for transfers between devices: 516 us -> 62.1 us
  matrix products: 142 us -> 0 us
  Pallas kernels: 0 us -> 71.2 us
  other arithmetic: 62.1 us -> 23.8 us
  blocking collectives: 36.4 us -> 56.7 us
  local copies, waits for them, and re-layouts: 41.8 us -> 60 us
  between operations: 16.7 us -> 1.2 us
  starting transfers between devices: 15.6 us -> 28.2 us
    reduce_scatter x6 -> x0, waiting for transfers between devices: 241 us -> none  [the longest x1 99.4 us: body(): lax.psum_scatter(grad_up, 'batch', scatter_dimension=0, tiled=True)]
    dot_general x41 -> x0, matrix products: 142 us -> none  [the longest x6 30.3 us: dot_plain(): return jnp.dot(matrix_a, matrix_b, preferred_element_type=jnp.float32)]
    ppermute x14 -> x26, waiting for transfers between devices: 197 us -> 62.1 us  [the longest x8 38.2 us: swap_first(): return lax.ppermute(array, ('blk', 'batch'), perm)]
    pallas_call x0 -> x3, Pallas kernels: none -> 71.2 us  [call(): pl.pallas_call(kernel, out_shape=[jax.ShapeDtypeStruct(s, d) for s, d in...]
    all_gather x2 -> x0, waiting for transfers between devices: 65.1 us -> none  [the longest x1 33 us: body(): lax.all_gather(values_local, 'blk', axis=1, tiled=True)]
    psum x1, blocking collectives: 9.99 us -> 56.7 us  [body(): mine = pick(lax.psum(stacked, ('blk', 'batch')), share)]
    convert_element_type x38 -> x12, other arithmetic: 44.9 us -> 13 us  [the longest x10 12.7 us: added(): return (a.astype(F32) + b.astype(F32)).astype(BF)]
    unnamed x1 -> x0, blocking collectives: 26.4 us -> none
  transfers between devices with their start and end apart: 23 -> 26, of which waited for: 21 -> 7; matrix products, arithmetic and copies ran while one was open for 17% -> 23% of each run, Pallas kernels for 0% -> 12%
where the time goes in v1:
time: 304 us; the launch traced here: 303 us
  Pallas kernels  71.2 us (23%)
  waiting for transfers between devices  62.1 us (20%)
  local copies, waits for them, and re-layouts  60 us (20%)
  blocking collectives  56.7 us (19%)
  starting transfers between devices  28.2 us (9%)
  other arithmetic  23.8 us (8%)
    pallas_call x3, Pallas kernels, call(): pl.pallas_call(kernel, out_shape=[jax.ShapeDtypeStruct(s, d) for s, d in...  71.2 us
    psum x1, blocking collectives, body(): mine = pick(lax.psum(stacked, ('blk', 'batch')), share)  56.7 us
    ppermute x8, waiting for transfers between devices, swap_first(): return lax.ppermute(array, ('blk', 'batch'), perm)  38.2 us
    ppermute x6, waiting for transfers between devices, swap_batch(): lax.ppermute(array, 'batch', [(i, i ^ bit) for i in range(lax.axis_size('...  23.9 us
    ppermute x12, starting transfers between devices, swap(): lax.ppermute(array, 'blk', [(i, i ^ bit) for i in range(lax.axis_size('bl...  15.5 us
    convert_element_type x10, other arithmetic, added(): return (a.astype(F32) + b.astype(F32)).astype(BF)  12.7 us
    gather x1, local copies, waits for them, and re-layouts, body(): jnp.take(table, jnp.pad(pick(token_ids, blk), (0, 128 - slots)), axis=0)  11.7 us
    squeeze x9, local copies, waits for them, and re-layouts, pick(): return lax.dynamic_index_in_dim(array, index, 0, keepdims=False)  10 us
  transfers between devices with their start and end apart: 26, of which 7 were waited for; matrix products, arithmetic and copies ran while one was open for 23% of the time, Pallas kernels for 12%

profile of v1, /device:TPU:0, one launch (start us, length us, event | category | flops | bytes accessed | tf_op | source)
XLA Modules:
  0.0 303.3 jit_solution(9970755481504567851)
XLA Ops:
  0.8 2.0 dynamic-slice_bitcast_fusion.16
  2.8 2.9 collective-permute-start
  7.2 1.9 dynamic-slice_bitcast_fusion.12
  9.2 2.0 collective-permute-start.3
  20.4 11.7 %gather_fusion = bf16[128,768]{1,0:T(8,128)(2,1)S(1)} fusion(bf16[15360,768]{1,0:T(8,128)(2,1)} %param.27, s32[1024]{0:T(1024)S(1)} %pad_clamp_fusion), kind=kCustom, calls=%fused_computation | custom fusion | bytes 393728 | tf_op jit(solution)/shard_map/jit(_take)/gather | solution.py:378
  32.1 1.9 pad_add_fusion.info_ref
  35.6 15.2 %shard_map.341 = (bf16[512,768]{1,0:T(8,128)(2,1)}, bf16[512,768]{1,0:T(8,128)(2,1)}, bf16[512,768]{1,0:T(8,128)(2,1)}, bf16[512,768]{1,0:T(8,128)(2,1)}, bf16[7...) custom-call(s32[4]{0:T(128)} %pad_add_fusion.info_ref, ...), custom_call_target="tpu_custom_call" | custom-call | flops 5637144576 | bytes 5711376 | tf_op jit(solution)/shard_map/pallas_call | solution.py:260
  51.6 35.2 %shard_map.342 = (bf16[512,768]{1,0:T(8,128)(2,1)}, bf16[2,4,4,2,96,768]{5,4,3,2,1,0:T(8,128)(2,1)}, bf16[768,768]{1,0:T(8,128)(2,1)}, f32[512,768]{1,0:T(8,128)...) custom-call(s32[4]{0:T(128)} %pad_add_fusion.info_ref, ...), custom_call_target="tpu_custom_call" | custom-call | flops 15703474176 | bytes 14076944 | tf_op jit(solution)/shard_map/pallas_call | solution.py:260
  86.8 4.9 %slice_bitcast_fusion = bf16[4,4,2,96,768]{4,3,2,1,0:T(8,128)(2,1)} fusion(bf16[2,4,4,2,96,768]{5,4,3,2,1,0:T(8,128)(2,1)} %get-tuple-element.68), kind=kLoop, calls=%fused_computation.7 | loop fusion | bytes 9437184 | tf_op jit(solution)/shard_map/squeeze | solution.py:342
  91.7 20.8 %shard_map.343 = (bf16[2,4,4,96,768]{4,3,2,1,0:T(8,128)(2,1)}, f32[1,768]{1,0:T(1,128)}, f32[1,768]{1,0:T(1,128)}, bf16[512,768]{1,0:T(8,128)(2,1)}) custom-call(s32[4]{0:T(128)} %pad_add_fusion.info_ref, s32[1,128]{1,0:T(1,128)} %pad_bitcast_fusion.pos_ref, bf16[512,768]{1,0:T(8,128)(2,1)} %get-tuple-element.48.x_ref, ...), custom_call_target="tpu_custom_call" | custom-call | flops 11676942336 | bytes 10273296 | tf_op jit(solution)/shard_map/pallas_call | solution.py:260
  112.5 1.8 slice_bitcast_fusion.1
  114.9 5.5 %fusion = bf16[4,4,2,96,768]{4,3,2,1,0:T(8,128)(2,1)S(1)} fusion(bf16[4,4,2,96,768]{4,3,2,1,0:T(8,128)(2,1)} %collective-permute-done.19, bf16[2,4,4,2,96,768]{5,4,3,2,1,0:T(8,128)(2,1)} %get-tuple-element.68), kind=kLoop, calls=%fused_computation.2 | loop fusion | flops 9437184 | bytes 14155776 | tf_op jit(solution)/shard_map/convert_element_type | solution.py:325
  120.5 1.7 dynamic-slice_bitcast_fusion
  122.1 1.9 copy-done
  124.0 1.9 collective-permute-start.20
  125.9 2.4 fusion.2
  130.8 2.1 dynamic-slice_bitcast_fusion.9
  141.0 2.0 reduce.13
  153.0 56.7 %psum.7 = f32[8,1152]{1,0:T(8,128)} all-reduce(f32[8,1152]{1,0:T(8,128)} %concatenate.31), channel_id=1, replica_groups=mesh['blk'=4,'batch'=8] {'blk','batch'}, use_global_device_ids=true, to_apply=%region_0.1 | all-reduce | flops 9216 | bytes 73728 | tf_op jit(solution)/shard_map/psum | solution.py:419
  214.1 2.3 collective-permute-start.9
  218.0 2.4 fusion.1
  222.7 1.6 bitcast_dynamic-update-slice_fusion.5
  224.8 1.6 bitcast_dynamic-update-slice_fusion.4
  227.6 1.6 bitcast_dynamic-update-slice_fusion.3
  229.2 20.1 %collective-permute-done.14 = bf16[4,96,768]{2,1,0:T(8,128)(2,1)S(1)} collective-permute-done((bf16[4,96,768]{2,1,0:T(8,128)(2,1)S(1)}, bf16[4,96,768]{2,1,0:T(8,128)(2,1)S(1)}, u32[]{:S(2)}, u32[]{:S(2)}) %collective-permute-start.14) | collective-permute-done | bytes 589856 | tf_op jit(solution)/shard_map/ppermute | solution.py:317
  250.4 1.7 collective-permute-start.22
  252.1 7.1 %collective-permute-done.15 = bf16[2,96,768]{2,1,0:T(8,128)(2,1)S(1)} collective-permute-done((bf16[2,96,768]{2,1,0:T(8,128)(2,1)S(1)}, bf16[2,96,768]{2,1,0:T(8,128)(2,1)S(1)}, u32[]{:S(2)}, u32[]{:S(2)}) %collective-permute-start.15) | collective-permute-done | bytes 294944 | tf_op jit(solution)/shard_map/ppermute | solution.py:321
  259.9 11.8 %collective-permute-done.16 = bf16[1,96,768]{2,1,0:T(8,128)(2,1)S(1)} collective-permute-done((bf16[1,96,768]{2,1,0:T(8,128)(2,1)S(1)}, bf16[1,96,768]{2,1,0:T(8,128)(2,1)S(1)}, u32[]{:S(2)}, u32[]{:S(2)}) %collective-permute-start.16) | collective-permute-done | bytes 147488 | tf_op jit(solution)/shard_map/ppermute | solution.py:321
  273.6 3.4 %collective-permute-done.17 = bf16[96,768]{1,0:T(8,128)(2,1)S(1)} collective-permute-done((bf16[96,768]{1,0:T(8,128)(2,1)S(1)}, bf16[96,768]{1,0:T(8,128)(2,1)S(1)}, u32[]{:S(2)}, u32[]{:S(2)}) %collective-permute-start.17) | collective-permute-done | bytes 147488 | tf_op jit(solution)/shard_map/ppermute | solution.py:317
  278.1 5.0 %collective-permute-done.23 = bf16[1,2,96,768]{3,2,1,0:T(8,128)(2,1)S(1)} collective-permute-done((bf16[1,2,96,768]{3,2,1,0:T(8,128)(2,1)S(1)}, bf16[1,2,96,768]{3,2,1,0:T(8,128)(2,1)S(1)}, u32[]{:S(2)}, u32[]{:S(2)}) %collective-permute-start.23) | collective-permute-done | bytes 294944 | tf_op jit(solution)/shard_map/ppermute | solution.py:321
  283.9 6.7 %collective-permute-done.24 = bf16[2,96,768]{2,1,0:T(8,128)(2,1)S(1)} collective-permute-done((bf16[2,96,768]{2,1,0:T(8,128)(2,1)S(1)}, bf16[2,96,768]{2,1,0:T(8,128)(2,1)S(1)}, u32[]{:S(2)}, u32[]{:S(2)}) %collective-permute-start.24) | collective-permute-done | bytes 294944 | tf_op jit(solution)/shard_map/ppermute | solution.py:317
  292.7 7.9 %collective-permute-done.25 = bf16[2,2,96,768]{3,2,1,0:T(8,128)(2,1)S(1)} collective-permute-done((bf16[2,2,96,768]{3,2,1,0:T(8,128)(2,1)S(1)}, bf16[2,2,96,768]{3,2,1,0:T(8,128)(2,1)S(1)}, u32[]{:S(2)}, u32[]{:S(2)}) %collective-permute-start.25) | collective-permute-done | bytes 589856 | tf_op jit(solution)/shard_map/ppermute | solution.py:317
  (155 shorter events, 54.3 us)
Async XLA Ops:
  0.7 16.2 %copy-start.4 = (bf16[3072]{0:T(1024)(128)(2,1)S(1)}, bf16[3072]{0:T(1024)(128)(2,1)}, u32[]{:S(2)}) copy-start(bf16[3072]{0:T(1024)(128)(2,1)} %param.38) | copy-start | bytes 18436
  0.7 16.7 %copy-start.11 = (bf16[768]{0:T(1024)(128)(2,1)S(1)}, bf16[768]{0:T(1024)(128)(2,1)}, u32[]{:S(2)}) copy-start(bf16[768]{0:T(1024)(128)(2,1)} %param.40) | copy-start | bytes 4612
  0.7 17.3 %copy-start.12 = (bf16[768]{0:T(1024)(128)(2,1)S(1)}, bf16[768]{0:T(1024)(128)(2,1)}, u32[]{:S(2)}) copy-start(bf16[768]{0:T(1024)(128)(2,1)} %param.35) | copy-start | bytes 4612
  0.7 17.9 %copy-start.13 = (bf16[768]{0:T(1024)(128)(2,1)S(1)}, bf16[768]{0:T(1024)(128)(2,1)}, u32[]{:S(2)}) copy-start(bf16[768]{0:T(1024)(128)(2,1)} %param.36) | copy-start | bytes 4612
  0.7 18.5 %copy-start.14 = (bf16[768]{0:T(1024)(128)(2,1)S(1)}, bf16[768]{0:T(1024)(128)(2,1)}, u32[]{:S(2)}) copy-start(bf16[768]{0:T(1024)(128)(2,1)} %param.41) | copy-start | bytes 4612
  0.8 19.1 %copy-start.15 = (bf16[768]{0:T(1024)(128)(2,1)S(1)}, bf16[768]{0:T(1024)(128)(2,1)}, u32[]{:S(2)}) copy-start(bf16[768]{0:T(1024)(128)(2,1)} %param.42) | copy-start | bytes 4612
  2.8 32.0 %collective-permute-start = (bf16[128,768]{1,0:T(8,128)(2,1)S(1)}, bf16[128,768]{1,0:T(8,128)(2,1)S(1)}, u32[]{:S(2)}, u32[]{:S(2)}) collective-permute-start(bf16[128,768]{1,0:T(8,128)(2,1)S(1)} %get-tuple-element.90), channel_id=1, source_target_pairs={{0,8},{8,0},{16,24},{24,16},{1,9},{9,1},{17,25},{25,17},{2,10},{10... | collective-permute-start | bytes 589832 | tf_op jit(solution)/shard_map/ppermute | solution.py:307
  5.7 29.1 %collective-permute-start.1 = (bf16[128,768]{1,0:T(8,128)(2,1)S(1)}, bf16[128,768]{1,0:T(8,128)(2,1)S(1)}, u32[]{:S(2)}, u32[]{:S(2)}) collective-permute-start(bf16[128,768]{1,0:T(8,128)(2,1)S(1)} %get-tuple-element.92), channel_id=1, source_target_pairs={{0,16},{8,24},{16,0},{24,8},{1,17},{9,25},{17,1},{25,9},{2,18},{10... | collective-permute-start | bytes 589832 | tf_op jit(solution)/shard_map/ppermute | solution.py:307
  7.2 27.6 %collective-permute-start.2 = (bf16[128,768]{1,0:T(8,128)(2,1)S(1)}, bf16[128,768]{1,0:T(8,128)(2,1)S(1)}, u32[]{:S(2)}, u32[]{:S(2)}) collective-permute-start(bf16[128,768]{1,0:T(8,128)(2,1)S(1)} %get-tuple-element.89), channel_id=1, source_target_pairs={{0,24},{8,16},{16,8},{24,0},{1,25},{9,17},{17,9},{25,1},{2,26},{10... | collective-permute-start | bytes 589832 | tf_op jit(solution)/shard_map/ppermute | solution.py:307
  9.2 41.6 %collective-permute-start.3 = (bf16[128,768]{1,0:T(8,128)(2,1)S(1)}, bf16[128,768]{1,0:T(8,128)(2,1)S(1)}, u32[]{:S(2)}, u32[]{:S(2)}) collective-permute-start(bf16[128,768]{1,0:T(8,128)(2,1)S(1)} %get-tuple-element.86), channel_id=1, source_target_pairs={{0,8},{8,0},{16,24},{24,16},{1,9},{9,1},{17,25},{25,17},{2,10},{10... | collective-permute-start | bytes 589832 | tf_op jit(solution)/shard_map/ppermute | solution.py:307
  11.1 39.7 %collective-permute-start.4 = (bf16[128,768]{1,0:T(8,128)(2,1)S(1)}, bf16[128,768]{1,0:T(8,128)(2,1)S(1)}, u32[]{:S(2)}, u32[]{:S(2)}) collective-permute-start(bf16[128,768]{1,0:T(8,128)(2,1)S(1)} %get-tuple-element.88), channel_id=1, source_target_pairs={{0,16},{8,24},{16,0},{24,8},{1,17},{9,25},{17,1},{25,9},{2,18},{10... | collective-permute-start | bytes 589832 | tf_op jit(solution)/shard_map/ppermute | solution.py:307
  34.8 16.0 %collective-permute-start.5 = (bf16[128,768]{1,0:T(8,128)(2,1)S(1)}, bf16[128,768]{1,0:T(8,128)(2,1)S(1)}, u32[]{:S(2)}, u32[]{:S(2)}) collective-permute-start(bf16[128,768]{1,0:T(8,128)(2,1)S(1)} %get-tuple-element.85), channel_id=1, source_target_pairs={{0,24},{8,16},{16,8},{24,0},{1,25},{9,17},{17,9},{25,1},{2,26},{10... | collective-permute-start | bytes 589832 | tf_op jit(solution)/shard_map/ppermute | solution.py:307
  91.7 23.2 %collective-permute-start.19 = (bf16[4,4,2,96,768]{4,3,2,1,0:T(8,128)(2,1)}, bf16[4,4,2,96,768]{4,3,2,1,0:T(8,128)(2,1)}, u32[]{:S(2)}, u32[]{:S(2)}) collective-permute-start(bf16[4,4,2,96,768]{4,3,2,1,0:T(8,128)(2,1)} %slice_bitcast_fusion), channel_id=1, source_target_pairs={{0,1},{1,0},{2,3},{3,2},{4,5},{5,4},{6,7},{7,6},{8,9},{9,8},{10,11... | collective-permute-start | bytes 14155784 | tf_op jit(solution)/shard_map/ppermute | solution.py:321
  114.4 11.5 %collective-permute-start.12 = (bf16[4,4,96,768]{3,2,1,0:T(8,128)(2,1)S(1)}, bf16[4,4,96,768]{3,2,1,0:T(8,128)(2,1)}, u32[]{:S(2)}, u32[]{:S(2)}) collective-permute-start(bf16[4,4,96,768]{3,2,1,0:T(8,128)(2,1)S(1)} %slice_bitcast_fusion.1), channel_id=1, source_target_pairs={{0,1},{1,0},{2,3},{3,2},{4,5},{5,4},{6,7},{7,6},{8,9},{9,8},{10,11... | collective-permute-start | bytes 7077896 | tf_op jit(solution)/shard_map/ppermute | solution.py:321
  124.0 94.0 %collective-permute-start.20 = (bf16[2,4,2,96,768]{4,3,2,1,0:T(8,128)(2,1)}, bf16[2,4,2,96,768]{4,3,2,1,0:T(8,128)(2,1)}, u32[]{:S(2)}, u32[]{:S(2)}) collective-permute-start(bf16[2,4,2,96,768]{4,3,2,1,0:T(8,128)(2,1)} %dynamic-slice_bitcast_fusion), channel_id=1, source_target_pairs={{0,8},{1,17},{2,10},{3,19},{4,12},{5,21},{6,14},{7,23},{8,0},{9,25... | collective-permute-start | bytes 7077896 | tf_op jit(solution)/shard_map/ppermute | solution.py:317
  128.5 85.6 %collective-permute-start.13 = (bf16[2,4,96,768]{3,2,1,0:T(8,128)(2,1)S(1)}, bf16[2,4,96,768]{3,2,1,0:T(8,128)(2,1)}, u32[]{:S(2)}, u32[]{:S(2)}) collective-permute-start(bf16[2,4,96,768]{3,2,1,0:T(8,128)(2,1)S(1)} %dynamic-slice_bitcast_fusion.2), channel_id=1, source_target_pairs={{0,8},{1,17},{2,10},{3,19},{4,12},{5,21},{6,14},{7,23},{8,0},{9,25... | collective-permute-start | bytes 3538952 | tf_op jit(solution)/shard_map/ppermute | solution.py:317
  132.9 88.2 %collective-permute-start.6 = (bf16[128,768]{1,0:T(8,128)(2,1)}, bf16[128,768]{1,0:T(8,128)(2,1)}, u32[]{:S(2)}, u32[]{:S(2)}) collective-permute-start(bf16[128,768]{1,0:T(8,128)(2,1)} %get-tuple-element.83), channel_id=1, source_target_pairs={{0,8},{8,0},{16,24},{24,16},{1,9},{9,1},{17,25},{25,17},{2,10},{10... | collective-permute-start | bytes 589832 | tf_op jit(solution)/shard_map/ppermute | solution.py:307
  133.6 90.7 %collective-permute-start.7 = (bf16[128,768]{1,0:T(8,128)(2,1)}, bf16[128,768]{1,0:T(8,128)(2,1)}, u32[]{:S(2)}, u32[]{:S(2)}) collective-permute-start(bf16[128,768]{1,0:T(8,128)(2,1)} %get-tuple-element.82), channel_id=1, source_target_pairs={{0,16},{8,24},{16,0},{24,8},{1,17},{9,25},{17,1},{25,9},{2,18},{10... | collective-permute-start | bytes 589832 | tf_op jit(solution)/shard_map/ppermute | solution.py:307
  135.1 91.3 %collective-permute-start.8 = (bf16[128,768]{1,0:T(8,128)(2,1)}, bf16[128,768]{1,0:T(8,128)(2,1)}, u32[]{:S(2)}, u32[]{:S(2)}) collective-permute-start(bf16[128,768]{1,0:T(8,128)(2,1)} %get-tuple-element.81), channel_id=1, source_target_pairs={{0,24},{8,16},{16,8},{24,0},{1,25},{9,17},{17,9},{25,1},{2,26},{10... | collective-permute-start | bytes 589832 | tf_op jit(solution)/shard_map/ppermute | solution.py:307
  214.1 45.8 %collective-permute-start.9 = (bf16[128,768]{1,0:T(8,128)(2,1)S(1)}, bf16[128,768]{1,0:T(8,128)(2,1)S(1)}, u32[]{:S(2)}, u32[]{:S(2)}) collective-permute-start(bf16[128,768]{1,0:T(8,128)(2,1)S(1)} %get-tuple-element.79), channel_id=1, source_target_pairs={{0,8},{8,0},{16,24},{24,16},{1,9},{9,1},{17,25},{25,17},{2,10},{10... | collective-permute-start | bytes 589832 | tf_op jit(solution)/shard_map/ppermute | solution.py:307
  220.4 29.6 %collective-permute-start.21 = (bf16[4,2,96,768]{3,2,1,0:T(8,128)(2,1)S(1)}, bf16[4,2,96,768]{3,2,1,0:T(8,128)(2,1)S(1)}, u32[]{:S(2)}, u32[]{:S(2)}) collective-permute-start(bf16[4,2,96,768]{3,2,1,0:T(8,128)(2,1)S(1)} %dynamic-slice_bitcast_fusion.1), channel_id=1, source_target_pairs={{0,16},{1,9},{2,18},{3,11},{4,20},{5,13},{6,22},{7,15},{8,24},{9,1... | collective-permute-start | bytes 3538952 | tf_op jit(solution)/shard_map/ppermute | solution.py:317
  221.1 28.3 %collective-permute-start.14 = (bf16[4,96,768]{2,1,0:T(8,128)(2,1)S(1)}, bf16[4,96,768]{2,1,0:T(8,128)(2,1)S(1)}, u32[]{:S(2)}, u32[]{:S(2)}) collective-permute-start(bf16[4,96,768]{2,1,0:T(8,128)(2,1)S(1)} %dynamic-slice_bitcast_fusion.4), channel_id=1, source_target_pairs={{0,16},{1,9},{2,18},{3,11},{4,20},{5,13},{6,22},{7,15},{8,24},{9,1... | collective-permute-start | bytes 1769480 | tf_op jit(solution)/shard_map/ppermute | solution.py:317
  224.3 49.3 %collective-permute-start.10 = (bf16[128,768]{1,0:T(8,128)(2,1)S(1)}, bf16[128,768]{1,0:T(8,128)(2,1)S(1)}, u32[]{:S(2)}, u32[]{:S(2)}) collective-permute-start(bf16[128,768]{1,0:T(8,128)(2,1)S(1)} %get-tuple-element.78), channel_id=1, source_target_pairs={{0,16},{8,24},{16,0},{24,8},{1,17},{9,25},{17,1},{25,9},{2,18},{10... | collective-permute-start | bytes 589832 | tf_op jit(solution)/shard_map/ppermute | solution.py:307
  226.4 57.2 %collective-permute-start.11 = (bf16[128,768]{1,0:T(8,128)(2,1)S(1)}, bf16[128,768]{1,0:T(8,128)(2,1)S(1)}, u32[]{:S(2)}, u32[]{:S(2)}) collective-permute-start(bf16[128,768]{1,0:T(8,128)(2,1)S(1)} %get-tuple-element.77), channel_id=1, source_target_pairs={{0,24},{8,16},{16,8},{24,0},{1,25},{9,17},{17,9},{25,1},{2,26},{10... | collective-permute-start | bytes 589832 | tf_op jit(solution)/shard_map/ppermute | solution.py:307
  249.5 9.6 %collective-permute-start.15 = (bf16[2,96,768]{2,1,0:T(8,128)(2,1)S(1)}, bf16[2,96,768]{2,1,0:T(8,128)(2,1)S(1)}, u32[]{:S(2)}, u32[]{:S(2)}) collective-permute-start(bf16[2,96,768]{2,1,0:T(8,128)(2,1)S(1)} %dynamic-slice_bitcast_fusion.5), channel_id=1, source_target_pairs={{0,2},{1,3},{2,0},{3,1},{4,6},{5,7},{6,4},{7,5},{8,10},{9,11},{10,... | collective-permute-start | bytes 884744 | tf_op jit(solution)/shard_map/ppermute | solution.py:321
  250.4 22.8 %collective-permute-start.22 = (bf16[2,2,96,768]{3,2,1,0:T(8,128)(2,1)S(1)}, bf16[2,2,96,768]{3,2,1,0:T(8,128)(2,1)S(1)}, u32[]{:S(2)}, u32[]{:S(2)}) collective-permute-start(bf16[2,2,96,768]{3,2,1,0:T(8,128)(2,1)S(1)} %dynamic-slice_bitcast_fusion.3), channel_id=1, source_target_pairs={{0,2},{1,3},{2,0},{3,1},{4,6},{5,7},{6,4},{7,5},{8,10},{9,11},{10,... | collective-permute-start | bytes 1769480 | tf_op jit(solution)/shard_map/ppermute | solution.py:321
  259.3 12.4 %collective-permute-start.16 = (bf16[1,96,768]{2,1,0:T(8,128)(2,1)S(1)}, bf16[1,96,768]{2,1,0:T(8,128)(2,1)S(1)}, u32[]{:S(2)}, u32[]{:S(2)}) collective-permute-start(bf16[1,96,768]{2,1,0:T(8,128)(2,1)S(1)} %constant_dynamic-slice_fusion.2), channel_id=1, source_target_pairs={{0,4},{1,5},{2,6},{3,7},{4,0},{5,1},{6,2},{7,3},{8,12},{9,13},{10,... | collective-permute-start | bytes 442376 | tf_op jit(solution)/shard_map/ppermute | solution.py:321
  271.8 5.2 %collective-permute-start.17 = (bf16[96,768]{1,0:T(8,128)(2,1)S(1)}, bf16[96,768]{1,0:T(8,128)(2,1)S(1)}, u32[]{:S(2)}, u32[]{:S(2)}) collective-permute-start(bf16[96,768]{1,0:T(8,128)(2,1)S(1)} %bitcast.153), channel_id=1, source_target_pairs={{0,16},{1,9},{2,18},{3,11},{4,20},{5,13},{6,22},{7,15},{8,24},{9,1... | collective-permute-start | bytes 442376 | tf_op jit(solution)/shard_map/ppermute | solution.py:317
  273.4 9.6 %collective-permute-start.23 = (bf16[1,2,96,768]{3,2,1,0:T(8,128)(2,1)S(1)}, bf16[1,2,96,768]{3,2,1,0:T(8,128)(2,1)S(1)}, u32[]{:S(2)}, u32[]{:S(2)}) collective-permute-start(bf16[1,2,96,768]{3,2,1,0:T(8,128)(2,1)S(1)} %constant_dynamic-slice_fusion.1), channel_id=1, source_target_pairs={{0,4},{1,5},{2,6},{3,7},{4,0},{5,1},{6,2},{7,3},{8,12},{9,13},{10,... | collective-permute-start | bytes 884744 | tf_op jit(solution)/shard_map/ppermute | solution.py:321
  277.0 6.8 %collective-permute-start.18 = (bf16[2,96,768]{2,1,0:T(8,128)(2,1)S(1)}, bf16[2,96,768]{2,1,0:T(8,128)(2,1)S(1)}, u32[]{:S(2)}, u32[]{:S(2)}) collective-permute-start(bf16[2,96,768]{2,1,0:T(8,128)(2,1)S(1)} %maximum_select_fusion.5), channel_id=1, source_target_pairs={{0,8},{1,17},{2,10},{3,19},{4,12},{5,21},{6,14},{7,23},{8,0},{9,25... | collective-permute-start | bytes 884744 | tf_op jit(solution)/shard_map/ppermute | solution.py:317
  283.1 7.4 %collective-permute-start.24 = (bf16[2,96,768]{2,1,0:T(8,128)(2,1)S(1)}, bf16[2,96,768]{2,1,0:T(8,128)(2,1)S(1)}, u32[]{:S(2)}, u32[]{:S(2)}) collective-permute-start(bf16[2,96,768]{2,1,0:T(8,128)(2,1)S(1)} %bitcast.149), channel_id=1, source_target_pairs={{0,16},{1,9},{2,18},{3,11},{4,20},{5,13},{6,22},{7,15},{8,24},{9,1... | collective-permute-start | bytes 884744 | tf_op jit(solution)/shard_map/ppermute | solution.py:317
  290.6 9.9 %collective-permute-start.25 = (bf16[2,2,96,768]{3,2,1,0:T(8,128)(2,1)S(1)}, bf16[2,2,96,768]{3,2,1,0:T(8,128)(2,1)S(1)}, u32[]{:S(2)}, u32[]{:S(2)}) collective-permute-start(bf16[2,2,96,768]{3,2,1,0:T(8,128)(2,1)S(1)} %maximum_select_fusion.3), channel_id=1, source_target_pairs={{0,8},{1,17},{2,10},{3,19},{4,12},{5,21},{6,14},{7,23},{8,0},{9,25... | collective-permute-start | bytes 1769480 | tf_op jit(solution)/shard_map/ppermute | solution.py:317
  (18 other events, 126.3 us)
